TPU v7x, 32 devices: a whole 2x2x4 slice. The times are simulated.
32 devices in a mesh: leaf: 8 (over z, x), grp: 4 (over y, core).
Axes of the slice: x: 2, y: 2, z: 4, core: 2. Of those that a mesh axis runs over, the one named last changes fastest.
Arguments:
- hidden_states: bfloat16 [4, 1024, 2560], P('grp', 'leaf'), may hold values from -6 to 6
- query_rows: bfloat16 [4, 1024, 5120], P('grp', 'leaf'), may hold values from -170 to 170
- key_rows: bfloat16 [4, 1024, 512], P('grp', 'leaf'), may hold values from -7 to 7
- value_weight: bfloat16 [2560, 512], P(('leaf', 'grp')), may hold values from -0.125 to 0.125
- parent_links: int32 [4, 8], P('grp', 'leaf'), may hold values from -1 to 6, as said below
- out_grad: bfloat16 [4, 1024, 5120], P('grp', 'leaf'), may hold values from -6 to 6
Outputs:
- attended: bfloat16 [4, 1024, 5120], P('grp', 'leaf')
- query_grad: bfloat16 [4, 1024, 5120], P('grp', 'leaf')
- key_grad: bfloat16 [4, 1024, 512], P('grp', 'leaf')
- hidden_grad: bfloat16 [4, 1024, 2560], P('grp', 'leaf')
- weight_grad: float32 [2560, 512], P(('leaf', 'grp'))
Inputs may be any that keep to these rules, and one draw needn't show every extreme that they name: `parent_links`: entry 0 of each tree is -1 and every other entry names a lower index; no segment has more than 4 children, every segment is at most 3 steps from segment 0, and in every tree some segment is exactly 3 steps from it and segment 0 has exactly 4 children.
All inputs are finite; a program needn't handle non-finite values.
Results may differ from a plain program's by a relative error of at most 0.028.
Values may be sent and summed in bfloat16 or wider, within the bound.
A program may use at most 128 MiB of HBM per device.

v0:
```python
import jax
import jax.numpy as jnp
from jax import lax
from jax.sharding import PartitionSpec as P

HQ = 40
HK = 4
DH = 128


def chain_slots(parent_list, own_index):
    total = parent_list.shape[0]

    def parent_of(node_index):
        hit = jnp.arange(total, dtype=jnp.int32) == node_index
        found = jnp.sum(jnp.where(hit, parent_list, 0))
        return jnp.where(node_index >= 0, found, -1)

    first = parent_of(own_index)
    second = parent_of(first)
    third = parent_of(second)
    return jnp.stack([first, second, third])


def key_mask(ancestors, segment_len):
    valid = jnp.concatenate([ancestors >= 0, jnp.ones((1,), bool)])
    block_ok = jnp.repeat(valid, segment_len)[None, :]
    row_ids = jnp.arange(segment_len, dtype=jnp.int32)[:, None]
    col_ids = jnp.arange(4 * segment_len, dtype=jnp.int32)[None, :]
    causal = (col_ids < 3 * segment_len) | (col_ids - 3 * segment_len <= row_ids)
    return block_ok & causal


def segment_pass(query_seg, key_all, value_all, grad_seg, visible):
    segment_len = query_seg.shape[0]
    groups = HQ // HK
    scale_factor = 1.0 / DH**0.5
    query_heads = query_seg.reshape(segment_len, HK, groups, DH)
    key_heads = key_all.reshape(-1, HK, DH)
    value_heads = value_all.reshape(-1, HK, DH)
    grad_heads = grad_seg.reshape(segment_len, HK, groups, DH)
    scores = (
        jnp.einsum("rhgd,khd->hgrk", query_heads, key_heads, preferred_element_type=jnp.float32)
        * scale_factor
    )
    scores = jnp.where(visible, scores, -1e30)
    row_max = jnp.max(scores, axis=-1, keepdims=True)
    weights_exp = jnp.where(visible, jnp.exp(scores - row_max), 0.0)
    probs = weights_exp / jnp.sum(weights_exp, axis=-1, keepdims=True)
    probs_low = probs.astype(jnp.bfloat16)
    output = jnp.einsum(
        "hgrk,khd->rhgd", probs_low, value_heads, preferred_element_type=jnp.float32
    )
    output = output.reshape(segment_len, HQ * DH).astype(jnp.bfloat16)
    dprobs = jnp.einsum(
        "rhgd,khd->hgrk", grad_heads, value_heads, preferred_element_type=jnp.float32
    )
    delta = jnp.sum(probs * dprobs, axis=-1, keepdims=True)
    dscores = (probs * (dprobs - delta)).astype(jnp.bfloat16)
    query_grad = (
        jnp.einsum("hgrk,khd->rhgd", dscores, key_heads, preferred_element_type=jnp.float32)
        * scale_factor
    )
    query_grad = query_grad.reshape(segment_len, HQ * DH).astype(jnp.bfloat16)
    key_part = (
        jnp.einsum("hgrk,rhgd->khd", dscores, query_heads, preferred_element_type=jnp.float32)
        * scale_factor
    )
    value_part = jnp.einsum(
        "hgrk,rhgd->khd", probs_low, grad_heads, preferred_element_type=jnp.float32
    )
    grad_term = jnp.concatenate(
        [key_part.reshape(-1, HK * DH), value_part.reshape(-1, HK * DH)], axis=1
    )
    return (output, query_grad, grad_term)


def shards(hidden_states, query_rows, key_rows, value_weight, parent_links, out_grad):
    hidden_local = hidden_states[0]
    query_local = query_rows[0]
    key_local = key_rows[0]
    grad_local = out_grad[0]
    segment_len = hidden_local.shape[0]
    key_width = key_local.shape[1]
    parent_list = lax.all_gather(parent_links, "leaf", axis=1, tiled=True)[0]
    own_index = lax.axis_index("leaf")
    ancestors = chain_slots(parent_list, own_index)
    columns = hidden_local
    values = jnp.dot(
        columns,
        lax.all_gather(value_weight, ("leaf", "grp"), axis=0, tiled=True),
        preferred_element_type=jnp.float32,
    )
    values = values.astype(jnp.bfloat16)
    key_value = jnp.concatenate([key_local, values], axis=1)
    every_segment = lax.all_gather(key_value, "leaf", axis=0, tiled=True)
    fetched = jnp.concatenate(
        [
            lax.dynamic_slice_in_dim(
                every_segment, jnp.maximum(ancestors[i], 0) * segment_len, segment_len, 0
            )
            for i in range(3)
        ],
        axis=0,
    )
    gathered = jnp.concatenate([fetched, key_value], axis=0)
    output, query_grad, grad_term = segment_pass(
        query_local,
        gathered[:, :key_width],
        gathered[:, key_width:],
        grad_local,
        key_mask(ancestors, segment_len),
    )
    grad_low = grad_term.astype(jnp.bfloat16)
    owners = jnp.concatenate([ancestors, own_index[None]])
    grad_wide = grad_low.astype(jnp.float32)
    targets = (
        owners[:, None] * segment_len + jnp.arange(segment_len, dtype=jnp.int32)[None, :]
    ).reshape(-1)
    keep_rows = (
        jnp.repeat(owners >= 0, segment_len)
        & (targets >= 0)
        & (targets < segment_len * lax.axis_size("leaf"))
    )
    targets = jnp.where(keep_rows, targets, segment_len * lax.axis_size("leaf"))
    sums = lax.psum_scatter(
        jnp.zeros((segment_len * lax.axis_size("leaf"), grad_wide.shape[1]), grad_wide.dtype)
        .at[targets]
        .add(grad_wide, mode="drop")
        .astype(jnp.bfloat16),
        "leaf",
        scatter_dimension=0,
        tiled=True,
    ).astype(jnp.float32)
    key_grad = sums[:, :key_width].astype(jnp.bfloat16)
    value_grad = sums[:, key_width:].astype(jnp.bfloat16)
    columns = hidden_local
    weight_grad = lax.psum_scatter(
        lax.dot_general(
            columns, value_grad, (((0,), (0,)), ((), ())), preferred_element_type=jnp.float32
        ),
        ("leaf", "grp"),
        scatter_dimension=0,
        tiled=True,
    )
    hidden_grad = lax.dot_general(
        value_grad,
        lax.all_gather(value_weight, ("leaf", "grp"), axis=0, tiled=True),
        (((1,), (1,)), ((), ())),
        preferred_element_type=jnp.float32,
    )
    hidden_grad = hidden_grad.astype(jnp.bfloat16)
    return (output[None], query_grad[None], key_grad[None], hidden_grad[None], weight_grad)


def solution(mesh):
    placed = (
        P("grp", "leaf", None),
        P("grp", "leaf", None),
        P("grp", "leaf", None),
        P(("leaf", "grp"), None),
        P("grp", "leaf"),
        P("grp", "leaf", None),
    )
    return jax.shard_map(
        shards,
        mesh=mesh,
        in_specs=placed,
        out_specs=(
            P("grp", "leaf", None),
            P("grp", "leaf", None),
            P("grp", "leaf", None),
            P("grp", "leaf", None),
            P(("leaf", "grp"), None),
        ),
        check_vma=False,
    )
```

profile of v0, /device:TPU:0, one launch (start us, length us, event | category | flops | bytes accessed | tf_op | source)
XLA Modules:
  0.0 393.2 jit_solution(18350468431384175426)
XLA Ops:
  8.0 63.6 %all-gather.3.cloned.1.call-done = bf16[2560,512]{1,0:T(8,128)(2,1)} async-done(((bf16[80,512]{1,0:T(8,128)(2,1)}), bf16[2560,512]{1,0:T(8,128)(2,1)}) %all-gather.3.cloned.1.call-update) | async-done | bytes 2621456 | tf_op jit(solution)/shard_map/all_gather | solution.py:91
  71.7 2.2 convolution_convert_fusion.1
  76.7 10.4 %all-reduce = s32[8]{0:T(128)S(1)} all-reduce(s32[8]{0:T(128)S(1)} %bitcast_dynamic-update-slice_fusion), channel_id=1, replica_groups=mesh['leaf'=8,'grp'=4] {'leaf'}, use_global_device_ids=true, to_apply=%add | all-reduce | flops 8 | bytes 64 | tf_op jit(solution)/shard_map/squeeze | solution.py:85
  90.9 1.4 copy.45
  92.4 1.4 copy.50
  95.2 28.1 %all-gather.5.cloned.1.call-done = bf16[1024,1024]{1,0:T(8,128)(2,1)} async-done(((bf16[128,1024]{1,0:T(8,128)(2,1)}), bf16[1024,1024]{1,0:T(8,128)(2,1)}) %all-gather.5.cloned.1.call-update) | async-done | bytes 2097168 | tf_op jit(solution)/shard_map/all_gather | solution.py:96
  126.1 7.6 %fusion.49 = (f32[4,10,128]{2,1,0:T(8,128)S(1)}, f32[4,10,128,512]{2,3,1,0:T(8,128)}) fusion(pred[128,512]{0,1:T(8,128)(4,1)} %fusion.38, bf16[512,4,128,1]{0,2,3,1:T(8,128)(2,1)S(1)} %copy.68, bf16[128,4,10,128]{0,3,2,1:T(8,128)(2,1)S(1)} %bitcast.102), kind=kOutput, calls=%fused_computation.76 | convolution fusion | flops 684196352 | bytes 12406784 | tf_op jit(solution)/shard_map/sub | solution.py:48
  133.6 7.0 %fusion.24 = bf16[4,512,128]{1,2,0:T(8,128)(2,1)} fusion(bf16[128,4,10,128]{0,3,2,1:T(8,128)(2,1)} %bitcast.104, f32[4,10,128,512]{2,3,1,0:T(8,128)} %get-tuple-element.28, f32[4,10,128]{2,1,0:T(8,128)S(1)} %get-tuple-element.27), kind=kOutput, calls=%fused_computation.30 | convolution fusion | flops 676593664 | bytes 12341248 | tf_op jit(solution)/shard_map/hgrk,rhgd->khd/dot_general | solution.py:69
  140.6 1.3 copy.58
  141.9 5.5 %fusion.1 = (f32[4,10,128]{2,1,0:T(8,128)S(1)}, f32[4,512,128,10]{2,1,3,0:T(8,128)S(1)}) fusion(f32[4,10,128,512]{2,3,1,0:T(8,128)} %get-tuple-element.28, f32[4,10,128]{2,1,0:T(8,128)} %copy-done.10, bf16[128,4,10,128]{0,3,2,1:T(8,128)(2,1)} %bitcast.105, bf16[512,4,128,1]{2,1,0,3:T(4,128)(2,1)S(1)} %bitcast.107), kind=kOutput, calls=%fused_computation.4 | convolution fusion | flops 678947840 | bytes 22847488 | tf_op jit(solution)/shard_map/rhgd,khd->hgrk/dot_general | solution.py:55
  147.5 1.3 slice-done.1
  149.4 3.2 fusion.3
  152.7 2.6 fusion.23
  156.6 7.2 %scatter_custom_fusion = f32[1024,1024]{1,0:T(8,128)} fusion(s32[512]{0:T(512)S(1)} %bitcast.114, f32[]{:T(128)} %constant.8.clone.1, bf16[512,512]{1,0:T(8,128)(2,1)S(1)} %copy.58, bf16[]{:T(256)} %constant.48, bf16[512,512]{1,0:T(8,128)(2,1)S(1)} %copy.57), kind=kCustom, calls=%fused_computation.22 | custom fusion | flops 2621440 | bytes 5242886 | tf_op jit(solution)/shard_map/scatter-add | solution.py:129
  163.7 3.9 convert_element_type.64
  167.7 66.4 %reduce-scatter.5.cloned.1.call-done = bf16[128,1024]{1,0:T(8,128)(2,1)} async-done(((bf16[1024,1024]{1,0:T(8,128)(2,1)}), bf16[128,1024]{1,0:T(8,128)(2,1)}) %reduce-scatter.5.cloned.1.call-update) | async-done | bytes 262160 | tf_op jit(solution)/shard_map/reduce_scatter | solution.py:126
  234.0 4.1 %convolution_bitcast_fusion = f32[2560,512]{0,1:T(8,128)} fusion(bf16[1,128,2560]{2,1,0:T(8,128)(2,1)S(1)} %copy-done, bf16[128,1024]{1,0:T(8,128)(2,1)} %reduce-scatter.5.cloned.1.call-done), kind=kOutput, calls=%fused_computation.14 | convolution fusion | flops 335544320 | bytes 6029312 | tf_op jit(solution)/shard_map/dot_general | solution.py:139
  238.1 5.9 %copy.82 = f32[2560,512]{1,0:T(8,128)} copy(f32[2560,512]{0,1:T(8,128)} %convolution_bitcast_fusion) | data formatting | bytes 10485760
  245.1 5.0 %fusion.16 = bf16[4,128,10,128]{3,1,2,0:T(8,128)(2,1)S(1)} fusion(bf16[512,4,128,1]{2,1,0,3:T(4,128)(2,1)S(1)} %bitcast.108, f32[4,10,128,512]{2,3,1,0:T(8,128)} %get-tuple-element.28, f32[4,10,128]{2,1,0:T(8,128)S(1)} %copy-done.12), kind=kOutput, calls=%fused_computation.25 | convolution fusion | flops 676986880 | bytes 12341248 | tf_op jit(solution)/shard_map/hgrk,khd->rhgd/dot_general | solution.py:51
  250.1 1.4 copy.59
  251.5 4.6 %multiply_convert_fusion = bf16[4,128,10,128]{3,1,2,0:T(8,128)(2,1)} fusion(bf16[512,4,128,1]{0,2,3,1:T(8,128)(2,1)S(1)} %copy.68, bf16[4,10,128,512]{2,3,1,0:T(8,128)(2,1)} %copy-done.1), kind=kOutput, calls=%fused_computation.17 | convolution fusion | flops 672399360 | bytes 7077888 | tf_op jit(solution)/shard_map/hgrk,khd->rhgd/dot_general | solution.py:61
  256.1 2.6 copy.60
  259.4 1.8 fusion.8
  261.2 125.5 %reduce-scatter.7.cloned.1.call-done = f32[80,512]{1,0:T(8,128)} async-done(((f32[2560,512]{1,0:T(8,128)}), f32[80,512]{1,0:T(8,128)}) %reduce-scatter.7.cloned.1.call-update) | async-done | bytes 163856
  (68 shorter events, 12.6 us)
Async XLA Ops:
  7.2 64.5 %copy-start = (bf16[1,128,2560]{2,1,0:T(8,128)(2,1)S(1)}, bf16[1,128,2560]{2,1,0:T(8,128)(2,1)}, u32[]{:S(2)}) copy-start(bf16[1,128,2560]{2,1,0:T(8,128)(2,1)} %param.6) | copy-start | bytes 1966084
  7.2 68.2 %copy-start.13 = (u32[32]{0:T(128)S(1)}, u32[32]{0:T(128)}, u32[]{:S(2)}) copy-start(u32[32]{0:T(128)} %constant.44) | copy-start | bytes 388
  7.2 66.7 %copy-start.9 = (bf16[1,128,512]{2,1,0:T(8,128)(2,1)S(1)}, bf16[1,128,512]{2,1,0:T(8,128)(2,1)}, u32[]{:S(2)}) copy-start(bf16[1,128,512]{2,1,0:T(8,128)(2,1)} %param.8) | copy-start | bytes 393220
  7.2 83.7 %copy-start.3 = (bf16[1,128,5120]{2,1,0:T(8,128)(2,1)S(1)}, bf16[1,128,5120]{2,1,0:T(8,128)(2,1)}, u32[]{:S(2)}) copy-start(bf16[1,128,5120]{2,1,0:T(8,128)(2,1)} %param.7) | copy-start | bytes 3932164
  7.2 64.4 %all-gather.3.cloned.1.call-start = ((), (), s32[]{:S(2)}) async-start(), calls=%async_computation.2 | async-start | bytes 2703360 | tf_op jit(solution)/shard_map/all_gather | solution.py:91
  7.9 84.4 %copy-start.4 = (bf16[1,128,5120]{2,1,0:T(8,128)(2,1)S(1)}, bf16[1,128,5120]{2,1,0:T(8,128)(2,1)}, u32[]{:S(2)}) copy-start(bf16[1,128,5120]{2,1,0:T(8,128)(2,1)} %param.11) | copy-start | bytes 3932164
  8.0 115.3 %all-gather.5.cloned.1.call-start = ((), (), s32[]{:S(2)}) async-start(), calls=%async_computation.3 | async-start | bytes 2359296 | tf_op jit(solution)/shard_map/all_gather | solution.py:96
  74.7 159.4 %reduce-scatter.5.cloned.1.call-start = ((), (), s32[]{:S(2)}) async-start(), calls=%async_computation.4 | async-start | bytes 2359296 | tf_op jit(solution)/shard_map/reduce_scatter | solution.py:126
  124.6 1.5 copy-start.5
  133.6 7.0 %copy-start.10 = (f32[4,10,128]{2,1,0:T(8,128)}, f32[4,10,128]{2,1,0:T(8,128)S(1)}, u32[]{:S(2)}) copy-start(f32[4,10,128]{2,1,0:T(8,128)S(1)} %get-tuple-element.27) | copy-start | bytes 61444
  133.6 8.3 %copy-start.7 = (bf16[512,4,128]{2,1,0:T(4,128)(2,1)S(1)}, bf16[512,4,128]{2,1,0:T(4,128)(2,1)}, u32[]{:S(2)}) copy-start(bf16[512,4,128]{2,1,0:T(4,128)(2,1)} %reshape.151) | copy-start | bytes 1572868
  141.9 5.6 %slice-start = ((s8[10485760]{0:T(1024)(128)(4,1)}), s8[4194304]{0:T(1024)(128)(4,1)S(1)}, s32[]{:S(2)}) async-start(s8[10485760]{0:T(1024)(128)(4,1)} %bitcast.98), calls=%async_computation.6 | async-start | bytes 8388608
  141.9 6.9 %slice-start.1 = ((s8[10485760]{0:T(1024)(128)(4,1)}), s8[4194304]{0:T(1024)(128)(4,1)S(1)}, s32[]{:S(2)}) async-start(s8[10485760]{0:T(1024)(128)(4,1)} %bitcast.98), calls=%async_computation.7 | async-start | bytes 8388608
  141.9 7.5 %slice-start.2 = ((s8[10485760]{0:T(1024)(128)(4,1)}), s8[2097152]{0:T(1024)(128)(4,1)S(1)}, s32[]{:S(2)}) async-start(s8[10485760]{0:T(1024)(128)(4,1)} %bitcast.98), calls=%async_computation.8 | async-start | bytes 4194304
  141.9 7.5 %copy-start.11 = (f32[4,10,128]{2,1,0:T(8,128)S(1)}, f32[4,10,128]{2,1,0:T(8,128)}, u32[]{:S(2)}) copy-start(f32[4,10,128]{2,1,0:T(8,128)} %copy-done.10) | copy-start | bytes 61444
  152.7 2.6 copy-start.1
  167.6 219.1 %reduce-scatter.7.cloned.1.call-start = ((), (), s32[]{:S(2)}) async-start(), calls=%async_computation.5 | async-start | bytes 5406720
  244.0 1.0 copy-start.8
  244.0 1.0 copy-start.12
  251.5 7.1 %copy-start.6 = (bf16[128,1024]{1,0:T(8,128)(2,1)S(1)}, bf16[128,1024]{1,0:T(8,128)(2,1)}, u32[]{:S(2)}) copy-start(bf16[128,1024]{1,0:T(8,128)(2,1)} %reduce-scatter.5.cloned.1.call-done) | copy-start | bytes 786436
  256.1 3.2 copy-start.2
Sparse Core Ops, SparseCore 0:
  10.9 60.6 all-gather.2
  74.8 48.4 all-gather.4
  167.7 66.2 reduce-scatter.4
  244.2 142.4 reduce-scatter.6
where the time goes:
time: 394 us; the launch traced here: 393 us
  waiting for transfers between devices  284 us (72%)
  matrix products  40.4 us (10%)
  local copies, waits for them, and re-layouts  23 us (6%)
  other arithmetic  18.2 us (5%)
  between operations  16.6 us (4%)
  blocking collectives  10.4 us (3%)
    unnamed x5, waiting for transfers between devices  126 us
    reduce_scatter x1, waiting for transfers between devices, shards(): lax.psum_scatter(jnp.zeros((segment_len * lax.axis_size('leaf'), grad_wid...  66.4 us
    all_gather x1, waiting for transfers between devices, shards(): lax.all_gather(value_weight, ('leaf', 'grp'), axis=0, tiled=True)  63.6 us
    all_gather x1, waiting for transfers between devices, shards(): every_segment = lax.all_gather(key_value, 'leaf', axis=0, tiled=True)  28.1 us
    unnamed x43, local copies, waits for them, and re-layouts  17.1 us
    squeeze x1, blocking collectives, shards(): parent_list = lax.all_gather(parent_links, 'leaf', axis=1, tiled=True)[0]  10.4 us
  transfers between devices with their start and end apart: 4, of which 4 were waited for; matrix products, arithmetic and copies ran while one was open for 6% of the time, Pallas kernels for 0%

commit v1 on v0

--- a/solution.py
+++ b/solution.py
@@ -1,11 +1,511 @@
+import functools
+
 import jax
 import jax.numpy as jnp
 from jax import lax
+from jax.experimental import pallas as pl
+from jax.experimental.pallas import tpu as pltpu
 from jax.sharding import PartitionSpec as P
 
 HQ = 40
 HK = 4
 DH = 128
+MESH = pl.DeviceIdType.MESH
+NX = 2
+NC = 2
+VMEM_LIMIT = 56 * 1024 * 1024
+
+
+def nt(a, b):
+    return lax.dot_general(a, b, (((1,), (1,)), ((), ())), preferred_element_type=jnp.float32)
+
+
+def nn(a, b):
+    return jnp.dot(a, b, preferred_element_type=jnp.float32)
+
+
+def place():
+    leaf = lax.axis_index("leaf")
+    grp = lax.axis_index("grp")
+    return leaf, grp, leaf // NX, leaf % NX, grp // NC, grp % NC
+
+
+def remote(src, dst, send, recv, leaf, grp):
+    return pltpu.make_async_remote_copy(
+        src_ref=src,
+        dst_ref=dst,
+        send_sem=send,
+        recv_sem=recv,
+        device_id=(leaf, grp),
+        device_id_type=MESH,
+    )
+
+
+def greet(leaf, grp, n_leaf, n_grp):
+    barrier = pltpu.get_barrier_semaphore()
+    for step in range(1, n_leaf):
+        pl.semaphore_signal(
+            barrier, inc=1, device_id=(lax.rem(leaf + step, n_leaf), grp), device_id_type=MESH
+        )
+    for step in range(1, n_grp):
+        pl.semaphore_signal(
+            barrier, inc=1, device_id=(leaf, lax.rem(grp + step, n_grp)), device_id_type=MESH
+        )
+    pl.semaphore_wait(barrier, n_leaf + n_grp - 2)
+
+
+def gather_kernel(
+    n_leaf, n_grp,
+    parent_ref, w_ref, key_ref, hidden_ref,
+    w_all, key_all, value_all, parents,
+    own_parent, par_send, par_recv, wz_send, wz_recv, w_send, w_recv, c_send, c_recv,
+    kz_send, kz_recv, kx_send, kx_recv, vz_send, vz_recv, vx_send, vx_recv,
+):
+    leaf, grp, z, x, y, c = place()
+    nz = n_leaf // NX
+    x_peer, y_peer, c_peer = z * NX + (1 - x), (1 - y) * NC + c, y * NC + (1 - c)
+    half = w_ref.shape[1] // 2
+    low, high = pl.ds(0, half), pl.ds(half, half)
+    pending = []
+
+    own_parent[...] = jnp.full(own_parent.shape, parent_ref[0, 0], jnp.int32)
+    greet(leaf, grp, n_leaf, n_grp)
+
+    def start(copy):
+        copy.start()
+        pending.append(copy)
+        return copy
+
+    wz = []
+    for d in range(1, nz):
+        to = lax.rem(z + d, nz)
+        wz.append(
+            start(remote(w_ref, w_all.at[z, x, y, c], wz_send.at[d - 1], wz_recv.at[d - 1], to * NX + x, grp))
+        )
+    par = []
+    for d in range(1, n_leaf):
+        par.append(
+            start(
+                remote(
+                    own_parent, parents.at[leaf], par_send.at[d - 1], par_recv.at[d - 1],
+                    lax.rem(leaf + d, n_leaf), grp,
+                )
+            )
+        )
+    w_all[z, x, y, c] = w_ref[...]
+    key_all[leaf] = key_ref[...]
+    parents[leaf] = own_parent[...]
+
+    def up_copy(block, whole, sems, d):
+        return remote(block, whole.at[leaf], sems[0].at[d - 1], sems[1].at[d - 1], leaf + d * NX, grp)
+
+    def up_start(block, whole, sems):
+        for d in range(1, nz):
+            @pl.when(z + d < nz)
+            def _(d=d):
+                up_copy(block, whole, sems, d).start()
+
+    def across_copy(whole, sems, d):
+        slot = leaf - d * NX
+        return remote(whole.at[slot], whole.at[slot], sems[0].at[d], sems[1].at[d], x_peer, grp)
+
+    def across_own(block, whole, sems):
+        @pl.when(x == 0)
+        def _():
+            remote(block, whole.at[leaf], sems[0].at[0], sems[1].at[0], x_peer, grp).start()
+
+    def across_start(whole, up_sems, sems):
+        for d in range(1, nz):
+            @pl.when(z - d >= 0)
+            def _(d=d):
+                slot = leaf - d * NX
+                remote(whole.at[slot], whole.at[slot], up_sems[0].at[d - 1], up_sems[1].at[d - 1], leaf, grp).wait_recv()
+                across_copy(whole, sems, d).start()
+
+    def finish(block, whole, up_sems, sems):
+        for d in range(1, nz):
+            @pl.when(z - d >= 0)
+            def _(d=d):
+                slot = z * NX - d * NX + (1 - x)
+                remote(whole.at[slot], whole.at[slot], sems[0].at[d], sems[1].at[d], x_peer, grp).wait()
+
+            @pl.when(z + d < nz)
+            def _(d=d):
+                up_copy(block, whole, up_sems, d).wait_send()
+
+        @pl.when(x == 0)
+        def _():
+            remote(block, whole.at[leaf], sems[0].at[0], sems[1].at[0], x_peer, grp).wait_send()
+
+        @pl.when(x == 1)
+        def _():
+            remote(block, whole.at[x_peer], sems[0].at[0], sems[1].at[0], x_peer, grp).wait_recv()
+
+    for copy in wz:
+        copy.wait_recv()
+
+    column_a = w_all.at[:, x, y, c, :, low]
+    column_b = w_all.at[:, x, y, c, :, high]
+    first_a = start(remote(column_a, column_a, w_send.at[0], w_recv.at[0], x_peer, grp))
+    first_b = start(remote(column_b, column_b, w_send.at[1], w_recv.at[1], leaf, y_peer))
+    whole_c = w_all.at[:, x, y, c]
+    to_core = [start(remote(whole_c, whole_c, c_send.at[0], c_recv.at[0], leaf, c_peer))]
+    up_start(key_ref, key_all, (kz_send, kz_recv))
+
+    first_a.wait_recv()
+    plane_a = w_all.at[:, :, y, c, :, low]
+    second_a = start(remote(plane_a, plane_a, w_send.at[2], w_recv.at[2], leaf, y_peer))
+    first_b.wait_recv()
+    plane_b = w_all.at[:, x, :, c, :, high]
+    second_b = start(remote(plane_b, plane_b, w_send.at[3], w_recv.at[3], x_peer, grp))
+    got_a = w_all.at[:, 1 - x, y, c, :, low]
+    got_b = w_all.at[:, x, 1 - y, c, :, high]
+    to_core.append(start(remote(got_a, got_a, c_send.at[1], c_recv.at[1], leaf, c_peer)))
+    to_core.append(start(remote(got_b, got_b, c_send.at[2], c_recv.at[2], leaf, c_peer)))
+
+    second_a.wait_recv()
+    late_a = w_all.at[:, :, 1 - y, c, :, low]
+    to_core.append(start(remote(late_a, late_a, c_send.at[3], c_recv.at[3], leaf, c_peer)))
+    second_b.wait_recv()
+    late_b = w_all.at[:, 1 - x, :, c, :, high]
+    to_core.append(start(remote(late_b, late_b, c_send.at[4], c_recv.at[4], leaf, c_peer)))
+    across_own(key_ref, key_all, (kx_send, kx_recv))
+    across_start(key_all, (kz_send, kz_recv), (kx_send, kx_recv))
+    for copy in to_core:
+        copy.wait_recv()
+
+    weight = w_all[...].reshape(hidden_ref.shape[1], w_ref.shape[1])
+    value_all[leaf] = nn(hidden_ref[...], weight).astype(jnp.bfloat16)
+    value_own = value_all.at[leaf]
+    up_start(value_own, value_all, (vz_send, vz_recv))
+    across_own(value_own, value_all, (vx_send, vx_recv))
+    across_start(value_all, (vz_send, vz_recv), (vx_send, vx_recv))
+
+    finish(key_ref, key_all, (kz_send, kz_recv), (kx_send, kx_recv))
+    for copy in par:
+        copy.wait_recv()
+    finish(value_own, value_all, (vz_send, vz_recv), (vx_send, vx_recv))
+    for copy in pending:
+        copy.wait_send()
+
+
+def gather_call(parent, w, key, hidden, n_leaf, n_grp):
+    nz, ny = n_leaf // NX, n_grp // NC
+    vmem = pl.BlockSpec(memory_space=pltpu.VMEM)
+    dma = pltpu.SemaphoreType.DMA
+    return pl.pallas_call(
+        functools.partial(gather_kernel, n_leaf, n_grp),
+        out_shape=[
+            jax.ShapeDtypeStruct((nz, NX, ny, NC) + w.shape, w.dtype),
+            jax.ShapeDtypeStruct((n_leaf,) + key.shape, key.dtype),
+            jax.ShapeDtypeStruct((n_leaf,) + key.shape, key.dtype),
+            jax.ShapeDtypeStruct((n_leaf, 8, 128), jnp.int32),
+        ],
+        in_specs=[pl.BlockSpec(memory_space=pltpu.SMEM)] + [vmem] * 3,
+        out_specs=[vmem] * 4,
+        scratch_shapes=[pltpu.VMEM((8, 128), jnp.int32)]
+        + [dma((n_leaf - 1,))] * 2
+        + [dma((nz - 1,))] * 2
+        + [dma((4,))] * 2
+        + [dma((5,))] * 2
+        + ([dma((nz - 1,))] * 2 + [dma((nz,))] * 2) * 2,
+        compiler_params=pltpu.CompilerParams(
+            collective_id=0, has_side_effects=True, vmem_limit_bytes=VMEM_LIMIT
+        ),
+        cost_estimate=pl.CostEstimate(flops=2 * 128 * 2560 * 512, bytes_accessed=6000000, transcendentals=0),
+    )(parent, w, key, hidden)
+
+
+def ancestors_of(par, own):
+    first = par[own]
+    second = jnp.where(first >= 0, par[jnp.maximum(first, 0)], -1)
+    third = jnp.where(second >= 0, par[jnp.maximum(second, 0)], -1)
+    return first, second, third
+
+
+def attention_kernel(
+    par, own, q_ref, g_ref, k0, k1, k2, k3, v0, v1, v2, v3,
+    o_ref, dq_ref, dk_ref, dv_ref, bias,
+):
+    seg = q_ref.shape[0]
+    groups = HQ // HK
+    scale = 1.0 / DH**0.5
+    fold = scale * 1.4426950408889634
+    chain = ancestors_of(par, own[0])
+
+    @pl.when(pl.program_id(0) == 0)
+    def _():
+        for i in range(3):
+            bias[i * seg : (i + 1) * seg, :] = jnp.full(
+                (seg, 2 * seg), jnp.where(chain[i] >= 0, 0.0, -1e30), jnp.float32
+            )
+        col = lax.broadcasted_iota(jnp.int32, (seg, 2 * seg), 0)
+        row = lax.broadcasted_iota(jnp.int32, (seg, 2 * seg), 1)
+        row = jnp.where(row >= seg, row - seg, row)
+        bias[3 * seg :, :] = jnp.where(col <= row, 0.0, -1e30)
+
+    key = jnp.concatenate([k0[0], k1[0], k2[0], k3[0]], axis=0)
+    value = jnp.concatenate([v0[0], v1[0], v2[0], v3[0]], axis=0)
+    key_t = key.T
+    value_t = value.T
+    dk = jnp.zeros((4 * seg, DH), jnp.float32)
+    dv = jnp.zeros((4 * seg, DH), jnp.float32)
+    for pair in range(groups // 2):
+        one, two = slice(2 * pair * DH, (2 * pair + 1) * DH), slice((2 * pair + 1) * DH, (2 * pair + 2) * DH)
+        q = jnp.concatenate([q_ref[:, one], q_ref[:, two]], axis=0)
+        g = jnp.concatenate([g_ref[:, one], g_ref[:, two]], axis=0)
+        s = nt(key, q) * fold + bias[...]
+        e = jnp.exp2(s - jnp.max(s, axis=0, keepdims=True))
+        p = e * (1.0 / jnp.sum(e, axis=0, keepdims=True))
+        p_low = p.astype(jnp.bfloat16)
+        dp = nt(value, g)
+        delta = jnp.sum(p * dp, axis=0, keepdims=True)
+        ds = (p * (dp - delta)).astype(jnp.bfloat16)
+        o = nn(value_t, p_low).T.astype(jnp.bfloat16)
+        o_ref[:, one] = o[:seg]
+        o_ref[:, two] = o[seg:]
+        dq = (nn(key_t, ds) * scale).T.astype(jnp.bfloat16)
+        dq_ref[:, one] = dq[:seg]
+        dq_ref[:, two] = dq[seg:]
+        dk = dk + nn(ds, q)
+        dv = dv + nn(p_low, g)
+    dk_ref[...] = (dk * scale).reshape(dk_ref.shape).astype(jnp.bfloat16)
+    dv_ref[...] = dv.reshape(dv_ref.shape).astype(jnp.bfloat16)
+
+
+def attention_call(par, own, q, g, key_all, value_all):
+    seg = q.shape[0]
+    wide = q.shape[1] // HK
+
+    def slot(i):
+        def index(h, par, own):
+            return (jnp.maximum(ancestors_of(par, own[0])[i], 0), 0, h)
+        return pl.BlockSpec((1, seg, DH), index)
+
+    mine = pl.BlockSpec((1, seg, DH), lambda h, par, own: (own[0], 0, h))
+    kv = [slot(0), slot(1), slot(2), mine]
+    rows = pl.BlockSpec((seg, wide), lambda h, par, own: (0, h))
+    terms = pl.BlockSpec((4, seg, DH), lambda h, par, own: (0, 0, h))
+    term = jax.ShapeDtypeStruct((4, seg, HK * DH), jnp.bfloat16)
+    return pl.pallas_call(
+        attention_kernel,
+        out_shape=[jax.ShapeDtypeStruct(q.shape, q.dtype)] * 2 + [term] * 2,
+        grid_spec=pltpu.PrefetchScalarGridSpec(
+            num_scalar_prefetch=2,
+            grid=(HK,),
+            in_specs=[rows, rows] + kv + kv,
+            out_specs=[rows, rows, terms, terms],
+            scratch_shapes=[pltpu.VMEM((4 * seg, 2 * seg), jnp.float32)],
+        ),
+        compiler_params=pltpu.CompilerParams(vmem_limit_bytes=VMEM_LIMIT),
+        cost_estimate=pl.CostEstimate(
+            flops=12 * HQ * seg * 4 * seg * DH, bytes_accessed=7000000, transcendentals=HQ * seg * 4 * seg
+        ),
+    )(par, own, q, g, *([key_all] * 4), *([value_all] * 4))
+
+
+def reduce_kernel(
+    n_leaf, n_grp,
+    par, dk_ref, dv_ref, hidden_t, w_ref,
+    dkey, dhidden, dweight,
+    vx_out, kx_out, vx_in, kx_in, vz_out, kz_out, vz_in, kz_in, hid_all, dv_all,
+    part, px_out, px_in, pz_out, pz_in,
+    vx_send, vx_recv, kx_send, kx_recv, vz_send, vz_recv, kz_send, kz_recv,
+    h_send, h_recv, g_send, g_recv, px_send, px_recv, pz_send, pz_recv,
+):
+    leaf, grp, z, x, y, c = place()
+    nz = n_leaf // NX
+    x_peer, y_peer, c_peer = z * NX + (1 - x), (1 - y) * NC + c, y * NC + (1 - c)
+    f32, bf16 = jnp.float32, jnp.bfloat16
+    chain = ancestors_of(par, leaf)
+
+    def term(ref, target):
+        slot = jnp.where(chain[0] == target, 0, jnp.where(chain[1] == target, 1, 2))
+        hit = (chain[0] == target) | (chain[1] == target) | (chain[2] == target)
+        block = ref[slot]
+        return jnp.where(hit, block, jnp.zeros_like(block))
+
+    greet(leaf, grp, n_leaf, n_grp)
+
+    def x_copy(out, into, sems, t):
+        return remote(out.at[t], into.at[t], sems[0].at[t], sems[1].at[t], x_peer, grp)
+
+    v_sems, k_sems = (vx_send, vx_recv), (kx_send, kx_recv)
+    for ref, out, into, sems in ((dv_ref, vx_out, vx_in, v_sems), (dk_ref, kx_out, kx_in, k_sems)):
+        for t in range(nz):
+            @pl.when((t < z) | ((t == z) & (x == 1)))
+            def _(t=t, ref=ref, out=out, into=into, sems=sems):
+                out[t] = term(ref, t * NX + (1 - x))
+                x_copy(out, into, sems, t).start()
+
+    hidden = []
+    for d in range(1, n_grp):
+        to = lax.rem(grp + d, n_grp)
+        copy = remote(hidden_t.at[:, to], hid_all.at[d], h_send.at[d - 1], h_recv.at[d - 1], leaf, to)
+        copy.start()
+        hidden.append(copy)
+
+    def z_copy(out, into, sems, t):
+        return remote(out.at[t], into.at[z], sems[0].at[t], sems[1].at[z], t * NX + x, grp)
+
+    vz_sems, kz_sems = (vz_send, vz_recv), (kz_send, kz_recv)
+    for ref, out, into, sems, z_out, z_in, z_sems in (
+        (dv_ref, vx_out, vx_in, v_sems, vz_out, vz_in, vz_sems),
+        (dk_ref, kx_out, kx_in, k_sems, kz_out, kz_in, kz_sems),
+    ):
+        for t in range(nz - 1):
+            @pl.when(t < z)
+            def _(t=t, ref=ref, out=out, into=into, sems=sems, z_out=z_out, z_in=z_in, z_sems=z_sems):
+                x_copy(out, into, sems, t).wait_recv()
+                total = term(ref, t * NX + x).astype(f32) + into[t].astype(f32)
+                z_out[t] = total.astype(bf16)
+                z_copy(z_out, z_in, z_sems, t).start()
+
+    def owned(ref, out, into, sems, z_in, z_sems, store):
+        store(ref[3].astype(f32))
+
+        @pl.when(x == 0)
+        def _():
+            for t in range(nz):
+                @pl.when(t == z)
+                def _(t=t):
+                    x_copy(out, into, sems, t).wait_recv()
+                    store(into[t].astype(f32), True)
+
+        for t in range(1, nz):
+            @pl.when(t > z)
+            def _(t=t):
+                remote(z_in.at[t], z_in.at[t], z_sems[0].at[t - 1], z_sems[1].at[t], t * NX + x, grp).wait_recv()
+                store(z_in[t].astype(f32), True)
+
+    acc = part.at[0]
+
+    def keep(value, more=False):
+        acc[...] = acc[...] + value if more else value
+
+    owned(dv_ref, vx_out, vx_in, v_sems, vz_in, vz_sems, keep)
+    dv_low = acc[...].astype(bf16)
+    dv_all[grp] = dv_low
+    mine = dv_all.at[grp]
+    to_y = remote(mine, mine, g_send.at[0], g_recv.at[0], leaf, y_peer)
+    to_c = remote(mine, mine, g_send.at[1], g_recv.at[1], leaf, c_peer)
+    to_y.start()
+    to_c.start()
+
+    width = w_ref.shape[0] // 4
+    for i in range(2):
+        dhidden[:, i * width : (i + 1) * width] = nt(dv_low, w_ref[i * width : (i + 1) * width, :]).astype(bf16)
+
+    to_y.wait_recv()
+    theirs = dv_all.at[y_peer]
+    relay = remote(theirs, theirs, g_send.at[2], g_recv.at[2], leaf, c_peer)
+    relay.start()
+    for i in range(2, 4):
+        dhidden[:, i * width : (i + 1) * width] = nt(dv_low, w_ref[i * width : (i + 1) * width, :]).astype(bf16)
+    for copy in hidden:
+        copy.wait_recv()
+    to_c.wait_recv()
+    relay.wait_recv()
+
+    def partial_at(target):
+        total = nn(hidden_t[target, grp], dv_all[grp])
+        for d in range(1, n_grp):
+            total = total + nn(hid_all[d, target], dv_all[lax.rem(grp + n_grp - d, n_grp)])
+        return total
+
+    px = []
+    for t in range(nz):
+        px_out[t] = partial_at(t * NX + (1 - x)).astype(bf16)
+        copy = remote(px_out.at[t], px_in.at[t], px_send.at[t], px_recv.at[t], x_peer, grp)
+        copy.start()
+        px.append(copy)
+    pz = []
+    for d in range(1, nz):
+        t = lax.rem(z + d, nz)
+        pz_out[d - 1] = partial_at(t * NX + x).astype(bf16)
+    dweight[...] = partial_at(leaf)
+    for copy in px:
+        copy.wait_recv()
+    for d in range(1, nz):
+        t = lax.rem(z + d, nz)
+        pz_out[d - 1] = (pz_out[d - 1].astype(f32) + px_in[t].astype(f32)).astype(bf16)
+        copy = remote(pz_out.at[d - 1], pz_in.at[d - 1], pz_send.at[d - 1], pz_recv.at[d - 1], t * NX + x, grp)
+        copy.start()
+        pz.append(copy)
+    dweight[...] += px_in[z].astype(f32)
+
+    owned(dk_ref, kx_out, kx_in, k_sems, kz_in, kz_sems, keep)
+    dkey[...] = acc[...].astype(bf16)
+
+    for copy in pz:
+        copy.wait_recv()
+    for d in range(1, nz):
+        dweight[...] += pz_in[d - 1].astype(f32)
+
+    for out, into, sems in ((vx_out, vx_in, v_sems), (kx_out, kx_in, k_sems)):
+        for t in range(nz):
+            @pl.when((t < z) | ((t == z) & (x == 1)))
+            def _(t=t, out=out, into=into, sems=sems):
+                x_copy(out, into, sems, t).wait_send()
+    for out, into, sems in ((vz_out, vz_in, vz_sems), (kz_out, kz_in, kz_sems)):
+        for t in range(nz - 1):
+            @pl.when(t < z)
+            def _(t=t, out=out, into=into, sems=sems):
+                z_copy(out, into, sems, t).wait_send()
+    for copy in hidden + [to_y, to_c, relay] + px + pz:
+        copy.wait_send()
+
+
+def reduce_call(par, dk, dv, hidden_t, w, n_leaf, n_grp):
+    nz = n_leaf // NX
+    _, seg, width = dk.shape
+    rows = hidden_t.shape[2]
+    bf16 = jnp.bfloat16
+    vmem = pl.BlockSpec(memory_space=pltpu.VMEM)
+    dma = pltpu.SemaphoreType.DMA
+    block = lambda n: pltpu.VMEM((n, seg, width), bf16)
+    piece = lambda n: pltpu.VMEM((n, rows, width), bf16)
+    return pl.pallas_call(
+        functools.partial(reduce_kernel, n_leaf, n_grp),
+        out_shape=[
+            jax.ShapeDtypeStruct((seg, width), bf16),
+            jax.ShapeDtypeStruct((seg, w.shape[0]), bf16),
+            jax.ShapeDtypeStruct((rows, width), jnp.float32),
+        ],
+        in_specs=[pl.BlockSpec(memory_space=pltpu.SMEM)] + [vmem] * 4,
+        out_specs=[vmem] * 3,
+        scratch_shapes=[block(nz)] * 8
+        + [
+            pltpu.VMEM((n_grp, n_leaf, rows, seg), bf16),
+            block(n_grp),
+            pltpu.VMEM((1, seg, width), jnp.float32),
+            piece(nz), piece(nz), piece(nz - 1), piece(nz - 1),
+        ]
+        + [dma((nz,))] * 8
+        + [dma((n_grp - 1,))] * 2
+        + [dma((3,))] * 2
+        + [dma((nz,))] * 2
+        + [dma((nz - 1,))] * 2,
+        compiler_params=pltpu.CompilerParams(
+            collective_id=1, has_side_effects=True, vmem_limit_bytes=VMEM_LIMIT
+        ),
+        cost_estimate=pl.CostEstimate(flops=4 * 128 * 2560 * 512, bytes_accessed=8000000, transcendentals=0),
+    )(par, dk, dv, hidden_t, w)
+
+
+def fast_shards(n_leaf, n_grp, hidden_states, query_rows, key_rows, value_weight, parent_links, out_grad):
+    hidden = hidden_states[0]
+    own = lax.axis_index("leaf").astype(jnp.int32).reshape(1)
+    w_all, key_all, value_all, parents = gather_call(
+        parent_links, value_weight, key_rows[0], hidden, n_leaf, n_grp
+    )
+    par = parents[:, 0, 0]
+    rows, width = value_weight.shape
+    w = w_all.reshape(hidden.shape[1], width)
+    hidden_t = hidden.T.reshape(n_leaf, n_grp, rows, hidden.shape[0])
+    out, dq, dk, dv = attention_call(par, own, query_rows[0], out_grad[0], key_all, value_all)
+    dkey, dhidden, dweight = reduce_call(par, dk, dv, hidden_t, w, n_leaf, n_grp)
+    return out[None], dq[None], dkey[None], dhidden[None], dweight
 
 
 def chain_slots(parent_list, own_index):
@@ -162,8 +662,16 @@
         P("grp", "leaf"),
         P("grp", "leaf", None),
     )
+    n_leaf, n_grp = mesh.shape["leaf"], mesh.shape["grp"]
+
+    def body(hidden_states, query_rows, key_rows, value_weight, parent_links, out_grad):
+        args = (hidden_states, query_rows, key_rows, value_weight, parent_links, out_grad)
+        if n_leaf % NX == 0 and n_grp == 2 * NC and value_weight.shape[0] % 16 == 0:
+            return fast_shards(n_leaf, n_grp, *args)
+        return shards(*args)
+
     return jax.shard_map(
-        shards,
+        body,
         mesh=mesh,
         in_specs=placed,
         out_specs=(

time: 394 us -> 129 us (0.33)
  waiting for transfers between devices: 284 us -> 0 us
  Pallas kernels: 0 us -> 120 us
  matrix products: 40.4 us -> 0 us
  other arithmetic: 18.2 us -> 0 us
  local copies, waits for them, and re-layouts: 23 us -> 6.83 us
  between operations: 16.6 us -> 1.32 us
  blocking collectives: 10.4 us -> 0 us
    unnamed x5 -> x0, waiting for transfers between devices: 126 us -> none
    pallas_call x0 -> x3, Pallas kernels: none -> 120 us  [the longest x1 63.8 us: reduce_call(): pl.pallas_call(functools.partial(reduce_kernel, n_leaf, n_grp), out_shape...]
    all_gather x2 -> x0, waiting for transfers between devices: 91.7 us -> none  [the longest x1 63.6 us: shards(): lax.all_gather(value_weight, ('leaf', 'grp'), axis=0, tiled=True)]
    reduce_scatter x1 -> x0, waiting for transfers between devices: 66.4 us -> none  [shards(): lax.psum_scatter(jnp.zeros((segment_len * lax.axis_size('leaf'), grad_wid...]
    dot_general x8 -> x0, matrix products: 32.9 us -> none  [the longest x1 6.98 us: segment_pass(): jnp.einsum('hgrk,rhgd->khd', probs_low, grad_heads, preferred_element_typ...]
    unnamed x43 -> x7, local copies, waits for them, and re-layouts: 17.1 us -> 4.24 us
    squeeze x1 -> x0, blocking collectives: 10.4 us -> none  [shards(): parent_list = lax.all_gather(parent_links, 'leaf', axis=1, tiled=True)[0]]
    sub x1 -> x0, matrix products: 7.56 us -> none  [segment_pass(): weights_exp = jnp.where(visible, jnp.exp(scores - row_max), 0.0)]
  transfers between devices with their start and end apart: 4 -> 0, of which waited for: 4 -> 0; matrix products, arithmetic and copies ran while one was open for 6% -> 0% of each run, Pallas kernels for 0% -> 0%
where the time goes in v1:
time: 129 us; the launch traced here: 128 us
  Pallas kernels  120 us (93%)
  local copies, waits for them, and re-layouts  6.83 us (5%)
  between operations  1.32 us (1%)
    pallas_call x1, Pallas kernels, reduce_call(): pl.pallas_call(functools.partial(reduce_kernel, n_leaf, n_grp), out_shape...  63.8 us
    pallas_call x1, Pallas kernels, gather_call(): pl.pallas_call(functools.partial(gather_kernel, n_leaf, n_grp), out_shape...  38 us
    pallas_call x1, Pallas kernels, attention_call(): pl.pallas_call(attention_kernel, out_shape=[jax.ShapeDtypeStruct(q.shape,...  17.9 us
    unnamed x7, local copies, waits for them, and re-layouts  4.24 us

profile of v1, /device:TPU:0, one launch (start us, length us, event | category | flops | bytes accessed | tf_op | source)
XLA Modules:
  0.0 127.8 jit_solution(9496528447063636657)
XLA Ops:
  1.3 38.0 %shard_map.101 = (bf16[4,2,2,2,80,512]{5,4,3,2,1,0:T(8,128)(2,1)}, bf16[8,128,512]{2,1,0:T(8,128)(2,1)}, bf16[8,128,512]{2,1,0:T(8,128)(2,1)}, s32[8,8,128]{2,1,0:T(8,128)}) custom-call(s32[1,1]{1,0:T(1,128)S(6)} %copy.16.parent_ref, bf16[80,512]{1,0:T(8,128)(2,1)} %w_ref.1, bf16[128,512]{1,0:T(8,128)(2,1)} %bitcast.21, bf16[128,2560]{1,0:T(8,128)(2,1)} %bitcast.15), custom_call_target="tpu_custom_call" | custom-call | flops 335544320 | bytes 6000000 | tf_op jit(solution)/shard_map/pallas_call | solution.py:196
  39.3 1.5 %slice_reduce_fusion.par = s32[8]{0:T(128)} fusion(s32[8,8,128]{2,1,0:T(8,128)} %get-tuple-element.16), kind=kLoop, calls=%fused_computation | loop fusion | bytes 64 | tf_op jit(solution)/shard_map/slice | solution.py:502
  40.8 0.0 copy-start
  40.8 17.9 %shard_map.102 = (bf16[128,5120]{1,0:T(8,128)(2,1)}, bf16[128,5120]{1,0:T(8,128)(2,1)}, bf16[4,128,512]{2,1,0:T(8,128)(2,1)}, bf16[4,128,512]{2,1,0:T(8,128)(2,1)}) custom-call(s32[8]{0:T(128)} %slice_reduce_fusion.par, s32[1]{0:T(128)} %bitcast.2.own, bf16[128,5120]{1,0:T(8,128)(2,1)} %bitcast.19, bf16[128,5120]{1,0:T(8,128)(2,1)} %bitcast.20, ...), custom_call_target="tpu_custom_call" | custom-call | flops 4026531840 | bytes 7000000 | tf_op jit(solution)/shard_map/pallas_call | solution.py:290
  58.7 0.0 copy-done
  58.7 1.1 copy.12
  59.7 63.8 %shard_map.103 = (bf16[128,512]{1,0:T(8,128)(2,1)}, bf16[128,2560]{1,0:T(8,128)(2,1)}, f32[80,512]{1,0:T(8,128)}) custom-call(s32[8]{0:T(128)} %slice_reduce_fusion.par, bf16[4,128,512]{2,1,0:T(8,128)(2,1)} %get-tuple-element.21.dk_ref, bf16[4,128,512]{2,1,0:T(8,128)(2,1)} %get-tuple-element.22.dv_ref, bf16[8,4,80,128]{3,2,1,0:T(8,128)(2,1)} %bitcast.13, ...), custom_call_target="tpu_custom_call" | custom-call | flops 671088640 | bytes 8000000 | tf_op jit(solution)/shard_map/pallas_call | solution.py:468
  123.6 0.0 copy-start.1
  123.6 1.6 %copy.17 = bf16[1,128,512]{2,1,0:T(8,128)(2,1)} copy(bf16[1,128,512]{2,1,0:T(8,128)(2,1)} %bitcast.18) | data formatting | bytes 262144
  125.2 2.0 %copy.18 = bf16[1,128,2560]{2,1,0:T(8,128)(2,1)} copy(bf16[1,128,2560]{2,1,0:T(8,128)(2,1)} %bitcast.17) | data formatting | bytes 1310720
  127.2 0.0 copy-done.1
  127.2 0.7 copy.19
Async XLA Ops:
  40.8 17.9 %copy-start = (bf16[1,128,2560]{2,1,0:T(8,128)(2,1)S(1)}, bf16[1,128,2560]{2,1,0:T(8,128)(2,1)}, u32[]{:S(2)}) copy-start(bf16[1,128,2560]{2,1,0:T(8,128)(2,1)} %param.6) | copy-start | bytes 1966084
  123.6 3.6 %copy-start.1 = (f32[80,512]{1,0:T(8,128)S(1)}, f32[80,512]{1,0:T(8,128)}, u32[]{:S(2)}) copy-start(f32[80,512]{1,0:T(8,128)} %get-tuple-element.36) | copy-start | bytes 491524

commit v2 on v0

--- a/solution.py
+++ b/solution.py
@@ -1,11 +1,512 @@
+import functools
+
 import jax
 import jax.numpy as jnp
 from jax import lax
+from jax.experimental import pallas as pl
+from jax.experimental.pallas import tpu as pltpu
 from jax.sharding import PartitionSpec as P
 
 HQ = 40
 HK = 4
 DH = 128
+MESH = pl.DeviceIdType.MESH
+NX = 2
+NC = 2
+VMEM_LIMIT = 56 * 1024 * 1024
+
+
+def nt(a, b):
+    return lax.dot_general(a, b, (((1,), (1,)), ((), ())), preferred_element_type=jnp.float32)
+
+
+def nn(a, b):
+    return jnp.dot(a, b, preferred_element_type=jnp.float32)
+
+
+def place():
+    leaf = lax.axis_index("leaf")
+    grp = lax.axis_index("grp")
+    return leaf, grp, leaf // NX, leaf % NX, grp // NC, grp % NC
+
+
+def remote(src, dst, send, recv, leaf, grp):
+    return pltpu.make_async_remote_copy(
+        src_ref=src,
+        dst_ref=dst,
+        send_sem=send,
+        recv_sem=recv,
+        device_id=(leaf, grp),
+        device_id_type=MESH,
+    )
+
+
+def greet(leaf, grp, n_leaf, n_grp):
+    barrier = pltpu.get_barrier_semaphore()
+    for step in range(1, n_leaf):
+        pl.semaphore_signal(
+            barrier, inc=1, device_id=(lax.rem(leaf + step, n_leaf), grp), device_id_type=MESH
+        )
+    for step in range(1, n_grp):
+        pl.semaphore_signal(
+            barrier, inc=1, device_id=(leaf, lax.rem(grp + step, n_grp)), device_id_type=MESH
+        )
+    pl.semaphore_wait(barrier, n_leaf + n_grp - 2)
+
+
+def ancestors_of(par, own):
+    first = par[own, 0]
+    second = jnp.where(first >= 0, par[jnp.maximum(first, 0), 0], -1)
+    third = jnp.where(second >= 0, par[jnp.maximum(second, 0), 0], -1)
+    return first, second, third
+
+
+def tree_kernel(
+    n_leaf, n_grp,
+    parent_ref, w_ref, key_ref, hidden_ref, hidden_t, q_hbm, g_hbm,
+    out_ref, dq_ref, dkey, dhidden, dweight,
+    q_ref, g_ref, w_all, key_all, v0, v1, v2, v3, parents, own_parent, par, bias, terms,
+    x_out, x_in, z_out, z_in, acc, hid_all, dv_all, px_out, px_in, pz_out, pz_in,
+    load_sem, par_send, par_recv, wz_send, wz_recv, w_send, w_recv, c_send, c_recv,
+    kz_send, kz_recv, kx_send, kx_recv, vz_send, vz_recv, vx_send, vx_recv,
+    gx_send, gx_recv, gz_send, gz_recv, h_send, h_recv, d_send, d_recv,
+    px_send, px_recv, pz_send, pz_recv,
+):
+    leaf, grp, z, x, y, c = place()
+    nz = n_leaf // NX
+    seg = key_ref.shape[0]
+    f32, bf16 = jnp.float32, jnp.bfloat16
+    scale = 1.0 / DH**0.5
+    fold = scale * 1.4426950408889634
+    x_peer, y_peer, c_peer = z * NX + (1 - x), (1 - y) * NC + c, y * NC + (1 - c)
+    values = (v0, v1, v2, v3)
+    half = w_ref.shape[1] // 2
+    low, high = pl.ds(0, half), pl.ds(half, half)
+    pending = []
+
+    loads = [
+        pltpu.make_async_copy(q_hbm, q_ref, load_sem.at[0]),
+        pltpu.make_async_copy(g_hbm, g_ref, load_sem.at[1]),
+    ]
+    for load in loads:
+        load.start()
+    own_parent[...] = jnp.full(own_parent.shape, parent_ref[0, 0], jnp.int32)
+    greet(leaf, grp, n_leaf, n_grp)
+
+    def start(copy):
+        copy.start()
+        pending.append(copy)
+        return copy
+
+    wz = []
+    for d in range(1, nz):
+        to = lax.rem(z + d, nz)
+        wz.append(
+            start(remote(w_ref, w_all.at[z, x, y, c], wz_send.at[d - 1], wz_recv.at[d - 1], to * NX + x, grp))
+        )
+    links = []
+    for d in range(1, n_leaf):
+        to = lax.rem(leaf + d, n_leaf)
+        links.append(
+            start(remote(own_parent, parents.at[leaf], par_send.at[d - 1], par_recv.at[d - 1], to, grp))
+        )
+    w_all[z, x, y, c] = w_ref[...]
+    key_all[leaf] = key_ref[...]
+    parents[leaf] = own_parent[...]
+
+    def up_copy(block, whole, sems, d):
+        return remote(block, whole.at[leaf], sems[0].at[d - 1], sems[1].at[d - 1], leaf + d * NX, grp)
+
+    def up_start(block, whole, sems):
+        for d in range(1, nz):
+            @pl.when(z + d < nz)
+            def _(d=d):
+                up_copy(block, whole, sems, d).start()
+
+    def across_own(block, whole, sems):
+        @pl.when(x == 0)
+        def _():
+            remote(block, whole.at[leaf], sems[0].at[0], sems[1].at[0], x_peer, grp).start()
+
+    def across_copy(whole, sems, d):
+        slot = leaf - d * NX
+        return remote(whole.at[slot], whole.at[slot], sems[0].at[d], sems[1].at[d], x_peer, grp)
+
+    def across_start(whole, up_sems, sems):
+        for d in range(1, nz):
+            @pl.when(z - d >= 0)
+            def _(d=d):
+                slot = leaf - d * NX
+                remote(whole.at[slot], whole.at[slot], up_sems[0].at[d - 1], up_sems[1].at[d - 1], leaf, grp).wait_recv()
+                across_copy(whole, sems, d).start()
+
+    def across_ready(block, whole, sems):
+        for d in range(1, nz):
+            @pl.when(z - d >= 0)
+            def _(d=d):
+                slot = x_peer - d * NX
+                remote(whole.at[slot], whole.at[slot], sems[0].at[d], sems[1].at[d], x_peer, grp).wait_recv()
+
+        @pl.when(x == 1)
+        def _():
+            remote(block, whole.at[x_peer], sems[0].at[0], sems[1].at[0], x_peer, grp).wait_recv()
+
+    def sent(block, whole, up_sems, sems):
+        for d in range(1, nz):
+            @pl.when(z + d < nz)
+            def _(d=d):
+                up_copy(block, whole, up_sems, d).wait_send()
+
+            @pl.when(z - d >= 0)
+            def _(d=d):
+                across_copy(whole, sems, d).wait_send()
+
+        @pl.when(x == 0)
+        def _():
+            remote(block, whole.at[leaf], sems[0].at[0], sems[1].at[0], x_peer, grp).wait_send()
+
+    k_up, k_across = (kz_send, kz_recv), (kx_send, kx_recv)
+
+    for copy in wz:
+        copy.wait_recv()
+    column_a = w_all.at[:, x, y, c, :, low]
+    column_b = w_all.at[:, x, y, c, :, high]
+    first_a = start(remote(column_a, column_a, w_send.at[0], w_recv.at[0], x_peer, grp))
+    first_b = start(remote(column_b, column_b, w_send.at[1], w_recv.at[1], leaf, y_peer))
+    whole_c = w_all.at[:, x, y, c]
+    to_core = [start(remote(whole_c, whole_c, c_send.at[0], c_recv.at[0], leaf, c_peer))]
+    up_start(key_ref, key_all, k_up)
+
+    first_a.wait_recv()
+    plane_a = w_all.at[:, :, y, c, :, low]
+    second_a = start(remote(plane_a, plane_a, w_send.at[2], w_recv.at[2], leaf, y_peer))
+    first_b.wait_recv()
+    plane_b = w_all.at[:, x, :, c, :, high]
+    second_b = start(remote(plane_b, plane_b, w_send.at[3], w_recv.at[3], x_peer, grp))
+    got_a = w_all.at[:, 1 - x, y, c, :, low]
+    got_b = w_all.at[:, x, 1 - y, c, :, high]
+    to_core.append(start(remote(got_a, got_a, c_send.at[1], c_recv.at[1], leaf, c_peer)))
+    to_core.append(start(remote(got_b, got_b, c_send.at[2], c_recv.at[2], leaf, c_peer)))
+    second_a.wait_recv()
+    late_a = w_all.at[:, :, 1 - y, c, :, low]
+    to_core.append(start(remote(late_a, late_a, c_send.at[3], c_recv.at[3], leaf, c_peer)))
+    second_b.wait_recv()
+    late_b = w_all.at[:, 1 - x, :, c, :, high]
+    to_core.append(start(remote(late_b, late_b, c_send.at[4], c_recv.at[4], leaf, c_peer)))
+
+    across_own(key_ref, key_all, k_across)
+    across_start(key_all, k_up, k_across)
+    hidden = []
+    for d in range(1, n_grp):
+        to = lax.rem(grp + d, n_grp)
+        hidden.append(
+            start(remote(hidden_t.at[to], hid_all.at[d], h_send.at[d - 1], h_recv.at[d - 1], leaf, to))
+        )
+    for copy in to_core:
+        copy.wait_recv()
+
+    weight = w_all[...].reshape(hidden_ref.shape[1], w_ref.shape[1])
+
+    def v_sems(h):
+        return (vz_send.at[h], vz_recv.at[h]), (vx_send.at[h], vx_recv.at[h])
+
+    for part in range(2):
+        pair = nn(hidden_ref[...], weight[:, part * half : (part + 1) * half]).astype(bf16)
+        for i in range(HK // 2):
+            h = part * (HK // 2) + i
+            whole = values[h]
+            whole[leaf] = pair[:, i * DH : (i + 1) * DH]
+            up, across = v_sems(h)
+            up_start(whole.at[leaf], whole, up)
+            across_own(whole.at[leaf], whole, across)
+
+    for copy in links:
+        copy.wait_recv()
+    listing = pltpu.make_async_copy(parents.at[:, 0], par, load_sem.at[2])
+    listing.start()
+
+    def forward(h):
+        if h < HK:
+            up, across = v_sems(h)
+            across_start(values[h], up, across)
+
+    forward(0)
+    listing.wait()
+    chain = ancestors_of(par, leaf)
+    for i in range(3):
+        bias[i * seg : (i + 1) * seg, :] = jnp.full(
+            (seg, 2 * seg), jnp.where(chain[i] >= 0, 0.0, -1e30), f32
+        )
+    col = lax.broadcasted_iota(jnp.int32, (seg, 2 * seg), 0)
+    row = lax.broadcasted_iota(jnp.int32, (seg, 2 * seg), 1)
+    row = jnp.where(row >= seg, row - seg, row)
+    bias[3 * seg :, :] = jnp.where(col <= row, 0.0, -1e30)
+    across_ready(key_ref, key_all, k_across)
+    for load in loads:
+        load.wait()
+    forward(1)
+
+    def head(h, hook):
+        up, across = v_sems(h)
+        across_ready(values[h].at[leaf], values[h], across)
+        lanes = slice(h * DH, (h + 1) * DH)
+        slots = [jnp.maximum(chain[i], 0) for i in range(3)] + [leaf]
+        key = jnp.concatenate([key_all[slot, :, lanes] for slot in slots], axis=0)
+        value = jnp.concatenate([values[h][slot] for slot in slots], axis=0)
+        key_t = key.T
+        value_t = value.T
+        dk = jnp.zeros((4 * seg, DH), f32)
+        dv = jnp.zeros((4 * seg, DH), f32)
+        groups = HQ // HK
+        for pair in range(groups // 2):
+            at = (h * groups + 2 * pair) * DH
+            one, two = slice(at, at + DH), slice(at + DH, at + 2 * DH)
+            q = jnp.concatenate([q_ref[:, one], q_ref[:, two]], axis=0)
+            g = jnp.concatenate([g_ref[:, one], g_ref[:, two]], axis=0)
+            s = nt(key, q) * fold + bias[...]
+            e = jnp.exp2(s - jnp.max(s, axis=0, keepdims=True))
+            p = e * (1.0 / jnp.sum(e, axis=0, keepdims=True))
+            p_low = p.astype(bf16)
+            dp = nt(value, g)
+            delta = jnp.sum(p * dp, axis=0, keepdims=True)
+            ds = (p * (dp - delta)).astype(bf16)
+            o = nn(value_t, p_low).T.astype(bf16)
+            out_ref[:, one] = o[:seg]
+            out_ref[:, two] = o[seg:]
+            dq = (nn(key_t, ds) * scale).T.astype(bf16)
+            dq_ref[:, one] = dq[:seg]
+            dq_ref[:, two] = dq[seg:]
+            dk = dk + nn(ds, q)
+            dv = dv + nn(p_low, g)
+            if pair == 1:
+                hook()
+        for i in range(4):
+            terms[h, i, :, :DH] = (dk[i * seg : (i + 1) * seg] * scale).astype(bf16)
+            terms[h, i, :, DH:] = dv[i * seg : (i + 1) * seg].astype(bf16)
+
+    def term(h, target):
+        slot = jnp.where(chain[0] == target, 0, jnp.where(chain[1] == target, 1, 2))
+        hit = (chain[0] == target) | (chain[1] == target) | (chain[2] == target)
+        block = terms[h, slot]
+        return jnp.where(hit, block, jnp.zeros_like(block))
+
+    def x_copy(h, t):
+        return remote(x_out.at[h, t], x_in.at[h, t], gx_send.at[h, t], gx_recv.at[h, t], x_peer, grp)
+
+    def z_copy(h, t):
+        return remote(z_out.at[h, t], z_in.at[h, z], gz_send.at[h, t], gz_recv.at[h, z], t * NX + x, grp)
+
+    def x_stage(h):
+        for t in range(nz):
+            @pl.when((t < z) | ((t == z) & (x == 1)))
+            def _(t=t):
+                x_out[h, t] = term(h, t * NX + (1 - x))
+                x_copy(h, t).start()
+
+    def z_stage(h):
+        for t in range(nz - 1):
+            @pl.when(t < z)
+            def _(t=t):
+                x_copy(h, t).wait_recv()
+                total = term(h, t * NX + x).astype(f32) + x_in[h, t].astype(f32)
+                z_out[h, t] = total.astype(bf16)
+                z_copy(h, t).start()
+
+    def owned(h):
+        acc[...] = terms[h, 3].astype(f32)
+        for t in range(nz):
+            @pl.when((t == z) & (x == 0))
+            def _(t=t):
+                x_copy(h, t).wait_recv()
+                acc[...] += x_in[h, t].astype(f32)
+
+        for t in range(1, nz):
+            @pl.when(t > z)
+            def _(t=t):
+                block = z_in.at[h, t]
+                remote(block, block, gz_send.at[h, t], gz_recv.at[h, t], t * NX + x, grp).wait_recv()
+                acc[...] += z_in[h, t].astype(f32)
+
+        lanes = slice(h * DH, (h + 1) * DH)
+        dkey[:, lanes] = acc[:, :DH].astype(bf16)
+        dv_all[h // 2, grp, :, (h % 2) * DH : (h % 2 + 1) * DH] = acc[:, DH:].astype(bf16)
+
+    def spread(part):
+        mine = dv_all.at[part, grp]
+        to_y = start(remote(mine, mine, d_send.at[part, 0], d_recv.at[part, 0], leaf, y_peer))
+        to_c = start(remote(mine, mine, d_send.at[part, 1], d_recv.at[part, 1], leaf, c_peer))
+        return to_y, to_c
+
+    def relay(part, to_y):
+        to_y.wait_recv()
+        theirs = dv_all.at[part, y_peer]
+        return start(remote(theirs, theirs, d_send.at[part, 2], d_recv.at[part, 2], leaf, c_peer))
+
+    rows = hidden_t.shape[3]
+
+    def partials(part, side):
+        total = nn(hidden_t[grp, side].reshape(nz * rows, seg), dv_all[part, grp])
+        for d in range(1, n_grp):
+            owner = lax.rem(grp + n_grp - d, n_grp)
+            total = total + nn(hid_all[d, side].reshape(nz * rows, seg), dv_all[part, owner])
+        return total
+
+    def px_copy(part):
+        return remote(px_out.at[part], px_in.at[part], px_send.at[part], px_recv.at[part], x_peer, grp)
+
+    def weight_x(part):
+        total = partials(part, 1 - x).astype(bf16)
+        px_out[part] = total.reshape(nz, rows, half)
+        start(px_copy(part))
+        pz_out[part] = partials(part, x).reshape(nz, rows, half)
+
+    def weight_z(part):
+        px_copy(part).wait_recv()
+        copies = []
+        for d in range(1, nz):
+            t = lax.rem(z + d, nz)
+            px_out_z = pz_out[part, t] + px_in[part, t].astype(f32)
+            pz_in[part, 0, d - 1] = px_out_z.astype(bf16)
+            copies.append(
+                start(
+                    remote(
+                        pz_in.at[part, 0, d - 1], pz_in.at[part, 1, d - 1],
+                        pz_send.at[part, d - 1], pz_recv.at[part, d - 1], t * NX + x, grp,
+                    )
+                )
+            )
+        return copies
+
+    head(0, lambda: forward(2))
+    x_stage(0)
+    head(1, lambda: forward(3))
+    x_stage(1)
+    z_stage(0)
+    head(2, lambda: None)
+    x_stage(2)
+    z_stage(1)
+    head(3, lambda: None)
+    x_stage(3)
+    z_stage(2)
+    owned(0)
+    owned(1)
+    to_y, to_c = spread(0)
+    for copy in hidden:
+        copy.wait_recv()
+    z_stage(3)
+    relayed = relay(0, to_y)
+    to_c.wait_recv()
+    relayed.wait_recv()
+    weight_x(0)
+    owned(2)
+    owned(3)
+    to_y, to_c = spread(1)
+    width = hidden_ref.shape[1] // 4
+    weight = w_all[...].reshape(hidden_ref.shape[1], w_ref.shape[1])
+    dv_low = jnp.concatenate([dv_all[0, grp], dv_all[1, grp]], axis=1)
+    copies = weight_z(0)
+    relayed = relay(1, to_y)
+    to_c.wait_recv()
+    relayed.wait_recv()
+    weight_x(1)
+    for i in range(4):
+        dhidden[:, i * width : (i + 1) * width] = nt(dv_low, weight[i * width : (i + 1) * width, :]).astype(bf16)
+    copies += weight_z(1)
+    for copy in copies:
+        copy.wait_recv()
+    for part in range(2):
+        total = pz_out[part, z] + px_in[part, z].astype(f32)
+        for d in range(1, nz):
+            total = total + pz_in[part, 1, d - 1].astype(f32)
+        dweight[:, part * half : (part + 1) * half] = total
+
+    sent(key_ref, key_all, k_up, k_across)
+    for h in range(HK):
+        up, across = v_sems(h)
+        sent(values[h].at[leaf], values[h], up, across)
+        for t in range(nz):
+            @pl.when((t < z) | ((t == z) & (x == 1)))
+            def _(t=t, h=h):
+                x_copy(h, t).wait_send()
+        for t in range(nz - 1):
+            @pl.when(t < z)
+            def _(t=t, h=h):
+                z_copy(h, t).wait_send()
+    for copy in pending:
+        copy.wait_send()
+
+
+def fast_shards(n_leaf, n_grp, hidden_states, query_rows, key_rows, value_weight, parent_links, out_grad):
+    hidden, q, g, key = hidden_states[0], query_rows[0], out_grad[0], key_rows[0]
+    rows, width = value_weight.shape
+    seg, features = hidden.shape
+    nz, ny = n_leaf // NX, n_grp // NC
+    half = width // 2
+    bf16, f32 = jnp.bfloat16, jnp.float32
+    hidden_t = hidden.T.reshape(nz, NX, n_grp, rows, seg).transpose(2, 1, 0, 3, 4)
+    vmem = pl.BlockSpec(memory_space=pltpu.VMEM)
+    anywhere = pl.BlockSpec(memory_space=pl.ANY)
+    held, dma = pltpu.VMEM, pltpu.SemaphoreType.DMA
+    pairs = lambda *dims: [dma(dims)] * 2
+    out, dq, dkey, dhidden, dweight = pl.pallas_call(
+        functools.partial(tree_kernel, n_leaf, n_grp),
+        out_shape=[
+            jax.ShapeDtypeStruct(q.shape, bf16),
+            jax.ShapeDtypeStruct(q.shape, bf16),
+            jax.ShapeDtypeStruct(key.shape, bf16),
+            jax.ShapeDtypeStruct(hidden.shape, bf16),
+            jax.ShapeDtypeStruct(value_weight.shape, f32),
+        ],
+        in_specs=[pl.BlockSpec(memory_space=pltpu.SMEM)] + [vmem] * 4 + [anywhere] * 2,
+        out_specs=[vmem] * 5,
+        scratch_shapes=[
+            held(q.shape, bf16),
+            held(q.shape, bf16),
+            held((nz, NX, ny, NC, rows, width), bf16),
+            held((n_leaf, seg, width), bf16),
+        ]
+        + [held((n_leaf, seg, DH), bf16)] * HK
+        + [
+            held((n_leaf, 8, 128), jnp.int32),
+            held((8, 128), jnp.int32),
+            pltpu.SMEM((n_leaf, 128), jnp.int32),
+            held((4 * seg, 2 * seg), f32),
+            held((HK, 4, seg, 2 * DH), bf16),
+        ]
+        + [held((HK, nz, seg, 2 * DH), bf16)] * 4
+        + [
+            held((seg, 2 * DH), f32),
+            held((n_grp, NX, nz, rows, seg), bf16),
+            held((2, n_grp, seg, half), bf16),
+            held((2, nz, rows, half), bf16),
+            held((2, nz, rows, half), bf16),
+            held((2, nz, rows, half), f32),
+            held((2, 2, nz - 1, rows, half), bf16),
+            dma((3,)),
+        ]
+        + pairs(n_leaf - 1)
+        + pairs(nz - 1)
+        + pairs(4)
+        + pairs(5)
+        + pairs(nz - 1)
+        + pairs(nz)
+        + pairs(HK, nz - 1)
+        + pairs(HK, nz)
+        + pairs(HK, nz) * 2
+        + pairs(n_grp - 1)
+        + pairs(2, 3)
+        + pairs(2)
+        + pairs(2, nz - 1),
+        compiler_params=pltpu.CompilerParams(
+            collective_id=0, has_side_effects=True, vmem_limit_bytes=VMEM_LIMIT
+        ),
+        cost_estimate=pl.CostEstimate(
+            flops=12 * HQ * seg * 4 * seg * DH + 6 * seg * features * width,
+            bytes_accessed=10000000,
+            transcendentals=HQ * seg * 4 * seg,
+        ),
+    )(parent_links, value_weight, key, hidden, hidden_t, q, g)
+    return out[None], dq[None], dkey[None], dhidden[None], dweight
 
 
 def chain_slots(parent_list, own_index):
@@ -162,8 +663,16 @@
         P("grp", "leaf"),
         P("grp", "leaf", None),
     )
+    n_leaf, n_grp = mesh.shape["leaf"], mesh.shape["grp"]
+
+    def body(hidden_states, query_rows, key_rows, value_weight, parent_links, out_grad):
+        args = (hidden_states, query_rows, key_rows, value_weight, parent_links, out_grad)
+        if n_leaf % NX == 0 and n_grp == 2 * NC and value_weight.shape[0] % 16 == 0:
+            return fast_shards(n_leaf, n_grp, *args)
+        return shards(*args)
+
     return jax.shard_map(
-        shards,
+        body,
         mesh=mesh,
         in_specs=placed,
         out_specs=(

time: 394 us -> 104 us (0.26)
  waiting for transfers between devices: 284 us -> 0 us
  Pallas kernels: 0 us -> 94.8 us
  matrix products: 40.4 us -> 0 us
  other arithmetic: 18.2 us -> 0 us
  between operations: 16.6 us -> 1.31 us
  local copies, waits for them, and re-layouts: 23 us -> 8.09 us
  blocking collectives: 10.4 us -> 0 us
    unnamed x5 -> x0, waiting for transfers between devices: 126 us -> none
    pallas_call x0 -> x1, Pallas kernels: none -> 94.8 us  [fast_shards(): pl.pallas_call(functools.partial(tree_kernel, n_leaf, n_grp), out_shape=[...]
    all_gather x2 -> x0, waiting for transfers between devices: 91.7 us -> none  [the longest x1 63.6 us: shards(): lax.all_gather(value_weight, ('leaf', 'grp'), axis=0, tiled=True)]
    reduce_scatter x1 -> x0, waiting for transfers between devices: 66.4 us -> none  [shards(): lax.psum_scatter(jnp.zeros((segment_len * lax.axis_size('leaf'), grad_wid...]
    dot_general x8 -> x0, matrix products: 32.9 us -> none  [the longest x1 6.98 us: segment_pass(): jnp.einsum('hgrk,rhgd->khd', probs_low, grad_heads, preferred_element_typ...]
    unnamed x43 -> x13, local copies, waits for them, and re-layouts: 17.1 us -> 5.79 us
    squeeze x1 -> x0, blocking collectives: 10.4 us -> none  [shards(): parent_list = lax.all_gather(parent_links, 'leaf', axis=1, tiled=True)[0]]
    sub x1 -> x0, matrix products: 7.56 us -> none  [segment_pass(): weights_exp = jnp.where(visible, jnp.exp(scores - row_max), 0.0)]
  transfers between devices with their start and end apart: 4 -> 0, of which waited for: 4 -> 0; matrix products, arithmetic and copies ran while one was open for 6% -> 0% of each run, Pallas kernels for 0% -> 0%
where the time goes in v2:
time: 104 us
  Pallas kernels  94.8 us (91%)
  local copies, waits for them, and re-layouts  8.09 us (8%)
  between operations  1.31 us (1%)
    pallas_call x1, Pallas kernels, fast_shards(): pl.pallas_call(functools.partial(tree_kernel, n_leaf, n_grp), out_shape=[...  94.8 us
    unnamed x13, local copies, waits for them, and re-layouts  5.79 us

profile of v2, /device:TPU:0, one launch (start us, length us, event | category | flops | bytes accessed | tf_op | source)
XLA Modules:
  0.0 104.1 jit_solution(5390942632700397559)
XLA Ops:
  1.3 1.4 %copy.11 = bf16[2560,128]{1,0:T(8,128)(2,1)S(1)} copy(bf16[2560,128]{0,1:T(8,128)(2,1)} %bitcast.17) | data formatting | bytes 1310720 | tf_op jit(solution)/shard_map/transpose | solution.py:446
  2.7 0.9 copy.14
  3.6 94.8 %shard_map.101 = (bf16[128,5120]{1,0:T(8,128)(2,1)}, bf16[128,5120]{1,0:T(8,128)(2,1)}, bf16[128,512]{1,0:T(8,128)(2,1)}, bf16[128,2560]{1,0:T(8,128)(2,1)}, f32[80,512]{1,0:T(8,128)}) custom-call(s32[1,1]{1,0:T(1,128)S(6)} %copy.20.parent_ref, bf16[80,512]{1,0:T(8,128)(2,1)} %w_ref.1, bf16[128,512]{1,0:T(8,128)(2,1)} %bitcast.24, ...), custom_call_target="tpu_custom_call" | custom-call | flops 5033164800 | bytes 10000000 | tf_op jit(solution)/shard_map/pallas_call | solution.py:451
  98.3 0.0 copy-start
  98.4 2.6 %copy.21 = bf16[1,128,5120]{2,1,0:T(8,128)(2,1)} copy(bf16[1,128,5120]{2,1,0:T(8,128)(2,1)} %bitcast.16) | data formatting | bytes 2621440
  100.9 0.0 copy-done
  100.9 0.0 copy-start.3
  100.9 0.0 copy-start.1
  100.9 1.1 %copy.22 = bf16[1,128,5120]{2,1,0:T(8,128)(2,1)} copy(bf16[1,128,5120]{2,1,0:T(8,128)(2,1)S(1)} %bitcast.15) | data formatting | bytes 2621440
  102.0 0.0 copy-done.3
  102.0 0.0 copy-start.2
  102.0 0.7 copy.23
  102.6 0.0 copy-done.1
  102.6 0.8 copy.24
  103.5 0.0 copy-done.2
  103.5 0.7 copy.25
Async XLA Ops:
  98.3 2.6 %copy-start = (bf16[128,5120]{1,0:T(8,128)(2,1)S(1)}, bf16[128,5120]{1,0:T(8,128)(2,1)}, u32[]{:S(2)}) copy-start(bf16[128,5120]{1,0:T(8,128)(2,1)} %get-tuple-element.11) | copy-start | bytes 3932164
  100.9 1.1 %copy-start.3 = (bf16[128,512]{1,0:T(8,128)(2,1)S(1)}, bf16[128,512]{1,0:T(8,128)(2,1)}, u32[]{:S(2)}) copy-start(bf16[128,512]{1,0:T(8,128)(2,1)} %get-tuple-element.12) | copy-start | bytes 393220
  100.9 1.7 %copy-start.1 = (bf16[128,2560]{1,0:T(8,128)(2,1)S(1)}, bf16[128,2560]{1,0:T(8,128)(2,1)}, u32[]{:S(2)}) copy-start(bf16[128,2560]{1,0:T(8,128)(2,1)} %get-tuple-element.13) | copy-start | bytes 1966084
  102.0 1.5 %copy-start.2 = (f32[80,512]{1,0:T(8,128)S(1)}, f32[80,512]{1,0:T(8,128)}, u32[]{:S(2)}) copy-start(f32[80,512]{1,0:T(8,128)} %get-tuple-element.24) | copy-start | bytes 491524

commit v3 on v2

--- a/solution.py
+++ b/solution.py
@@ -63,9 +63,9 @@
 
 def tree_kernel(
     n_leaf, n_grp,
-    parent_ref, w_ref, key_ref, hidden_ref, hidden_t, q_hbm, g_hbm,
+    parent_ref, w_ref, key_ref, hidden_ref, q_hbm, g_hbm,
     out_ref, dq_ref, dkey, dhidden, dweight,
-    q_ref, g_ref, w_all, key_all, v0, v1, v2, v3, parents, own_parent, par, bias, terms,
+    q_ref, g_ref, hidden_t, w_all, key_all, v0, v1, v2, v3, parents, own_parent, par, bias, probs, terms,
     x_out, x_in, z_out, z_in, acc, hid_all, dv_all, px_out, px_in, pz_out, pz_in,
     load_sem, par_send, par_recv, wz_send, wz_recv, w_send, w_recv, c_send, c_recv,
     kz_send, kz_recv, kx_send, kx_recv, vz_send, vz_recv, vx_send, vx_recv,
@@ -81,7 +81,6 @@
     x_peer, y_peer, c_peer = z * NX + (1 - x), (1 - y) * NC + c, y * NC + (1 - c)
     values = (v0, v1, v2, v3)
     half = w_ref.shape[1] // 2
-    low, high = pl.ds(0, half), pl.ds(half, half)
     pending = []
 
     loads = [
@@ -98,12 +97,21 @@
         pending.append(copy)
         return copy
 
-    wz = []
-    for d in range(1, nz):
-        to = lax.rem(z + d, nz)
-        wz.append(
-            start(remote(w_ref, w_all.at[z, x, y, c], wz_send.at[d - 1], wz_recv.at[d - 1], to * NX + x, grp))
-        )
+    def w_over_z(part):
+        lanes = pl.ds(part * half, half)
+        copies = []
+        for d in range(1, nz):
+            copies.append(
+                start(
+                    remote(
+                        w_ref.at[:, lanes], w_all.at[z, x, y, c, :, lanes],
+                        wz_send.at[part, d - 1], wz_recv.at[part, d - 1], lax.rem(z + d, nz) * NX + x, grp,
+                    )
+                )
+            )
+        return copies
+
+    wz = w_over_z(0)
     links = []
     for d in range(1, n_leaf):
         to = lax.rem(leaf + d, n_leaf)
@@ -167,33 +175,83 @@
 
     k_up, k_across = (kz_send, kz_recv), (kx_send, kx_recv)
 
+    rows = hidden_t.shape[3]
+    for first in range(nz):
+        block = NX * n_grp * rows
+        turned = hidden_ref[:, first * block : (first + 1) * block].T
+        for i in range(NX):
+            for j in range(n_grp):
+                at = (i * n_grp + j) * rows
+                hidden_t[j, i, first] = turned[at : at + rows]
+
+    quarter = half // 2
+    to_core = [[], []]
+
+    def lanes_of(part):
+        return pl.ds(part * half, quarter), pl.ds(part * half + quarter, quarter)
+
+    def w_copy(part, i, block, leaf_to, grp_to):
+        return start(remote(block, block, w_send.at[part, i], w_recv.at[part, i], leaf_to, grp_to))
+
+    def w_core(part, i, block):
+        to_core[part].append(
+            start(remote(block, block, c_send.at[part, i], c_recv.at[part, i], leaf, c_peer))
+        )
+
+    def w_first(part):
+        a, b = lanes_of(part)
+        return (
+            w_copy(part, 0, w_all.at[:, x, y, c, :, a], x_peer, grp),
+            w_copy(part, 1, w_all.at[:, x, y, c, :, b], leaf, y_peer),
+        )
+
+    def w_second(part, first):
+        a, b = lanes_of(part)
+        first[0].wait_recv()
+        over_y = w_copy(part, 2, w_all.at[:, :, y, c, :, a], leaf, y_peer)
+        first[1].wait_recv()
+        over_x = w_copy(part, 3, w_all.at[:, x, :, c, :, b], x_peer, grp)
+        w_core(part, 0, w_all.at[:, x, y, c, :, pl.ds(part * half, half)])
+        w_core(part, 1, w_all.at[:, 1 - x, y, c, :, a])
+        w_core(part, 2, w_all.at[:, x, 1 - y, c, :, b])
+        return over_y, over_x
+
+    def w_third(part, second):
+        a, b = lanes_of(part)
+        second[0].wait_recv()
+        w_core(part, 3, w_all.at[:, :, 1 - y, c, :, a])
+        second[1].wait_recv()
+        w_core(part, 4, w_all.at[:, 1 - x, :, c, :, b])
+
+    def v_sems(h):
+        return (vz_send.at[h], vz_recv.at[h]), (vx_send.at[h], vx_recv.at[h])
+
+    def project(part):
+        for copy in to_core[part]:
+            copy.wait_recv()
+        weight = w_all[:, :, :, :, :, part * half : (part + 1) * half].reshape(hidden_ref.shape[1], half)
+        pair = nn(hidden_ref[...], weight).astype(bf16)
+        for i in range(HK // 2):
+            h = part * (HK // 2) + i
+            whole = values[h]
+            whole[leaf] = pair[:, i * DH : (i + 1) * DH]
+            up, across = v_sems(h)
+            up_start(whole.at[leaf], whole, up)
+            across_own(whole.at[leaf], whole, across)
+
     for copy in wz:
         copy.wait_recv()
-    column_a = w_all.at[:, x, y, c, :, low]
-    column_b = w_all.at[:, x, y, c, :, high]
-    first_a = start(remote(column_a, column_a, w_send.at[0], w_recv.at[0], x_peer, grp))
-    first_b = start(remote(column_b, column_b, w_send.at[1], w_recv.at[1], leaf, y_peer))
-    whole_c = w_all.at[:, x, y, c]
-    to_core = [start(remote(whole_c, whole_c, c_send.at[0], c_recv.at[0], leaf, c_peer))]
+    first0 = w_first(0)
+    wz = w_over_z(1)
+    second0 = w_second(0, first0)
+    for copy in wz:
+        copy.wait_recv()
+    first1 = w_first(1)
     up_start(key_ref, key_all, k_up)
-
-    first_a.wait_recv()
-    plane_a = w_all.at[:, :, y, c, :, low]
-    second_a = start(remote(plane_a, plane_a, w_send.at[2], w_recv.at[2], leaf, y_peer))
-    first_b.wait_recv()
-    plane_b = w_all.at[:, x, :, c, :, high]
-    second_b = start(remote(plane_b, plane_b, w_send.at[3], w_recv.at[3], x_peer, grp))
-    got_a = w_all.at[:, 1 - x, y, c, :, low]
-    got_b = w_all.at[:, x, 1 - y, c, :, high]
-    to_core.append(start(remote(got_a, got_a, c_send.at[1], c_recv.at[1], leaf, c_peer)))
-    to_core.append(start(remote(got_b, got_b, c_send.at[2], c_recv.at[2], leaf, c_peer)))
-    second_a.wait_recv()
-    late_a = w_all.at[:, :, 1 - y, c, :, low]
-    to_core.append(start(remote(late_a, late_a, c_send.at[3], c_recv.at[3], leaf, c_peer)))
-    second_b.wait_recv()
-    late_b = w_all.at[:, 1 - x, :, c, :, high]
-    to_core.append(start(remote(late_b, late_b, c_send.at[4], c_recv.at[4], leaf, c_peer)))
-
+    w_third(0, second0)
+    second1 = w_second(1, first1)
+    project(0)
+    w_third(1, second1)
     across_own(key_ref, key_all, k_across)
     across_start(key_all, k_up, k_across)
     hidden = []
@@ -202,24 +260,7 @@
         hidden.append(
             start(remote(hidden_t.at[to], hid_all.at[d], h_send.at[d - 1], h_recv.at[d - 1], leaf, to))
         )
-    for copy in to_core:
-        copy.wait_recv()
-
-    weight = w_all[...].reshape(hidden_ref.shape[1], w_ref.shape[1])
-
-    def v_sems(h):
-        return (vz_send.at[h], vz_recv.at[h]), (vx_send.at[h], vx_recv.at[h])
-
-    for part in range(2):
-        pair = nn(hidden_ref[...], weight[:, part * half : (part + 1) * half]).astype(bf16)
-        for i in range(HK // 2):
-            h = part * (HK // 2) + i
-            whole = values[h]
-            whole[leaf] = pair[:, i * DH : (i + 1) * DH]
-            up, across = v_sems(h)
-            up_start(whole.at[leaf], whole, up)
-            across_own(whole.at[leaf], whole, across)
-
+    project(1)
     for copy in links:
         copy.wait_recv()
     listing = pltpu.make_async_copy(parents.at[:, 0], par, load_sem.at[2])
@@ -230,7 +271,6 @@
             up, across = v_sems(h)
             across_start(values[h], up, across)
 
-    forward(0)
     listing.wait()
     chain = ancestors_of(par, leaf)
     for i in range(3):
@@ -244,28 +284,39 @@
     across_ready(key_ref, key_all, k_across)
     for load in loads:
         load.wait()
-    forward(1)
-
-    def head(h, hook):
+
+    groups = HQ // HK
+    slots = [jnp.maximum(chain[i], 0) for i in range(3)] + [leaf]
+
+    def places(h, pair):
+        at = (h * groups + 2 * pair) * DH
+        return slice(at, at + DH), slice(at + DH, at + 2 * DH)
+
+    def keys_of(h):
+        return jnp.concatenate([key_all[slot, :, h * DH : (h + 1) * DH] for slot in slots], axis=0)
+
+    def softmax(h):
+        key = keys_of(h)
+        for pair in range(groups // 2):
+            one, two = places(h, pair)
+            q = jnp.concatenate([q_ref[:, one], q_ref[:, two]], axis=0)
+            s = nt(key, q) * fold + bias[...]
+            e = jnp.exp2(s - jnp.max(s, axis=0, keepdims=True))
+            probs[h * (groups // 2) + pair] = e * (1.0 / jnp.sum(e, axis=0, keepdims=True))
+
+    def gradients(h):
         up, across = v_sems(h)
         across_ready(values[h].at[leaf], values[h], across)
-        lanes = slice(h * DH, (h + 1) * DH)
-        slots = [jnp.maximum(chain[i], 0) for i in range(3)] + [leaf]
-        key = jnp.concatenate([key_all[slot, :, lanes] for slot in slots], axis=0)
         value = jnp.concatenate([values[h][slot] for slot in slots], axis=0)
-        key_t = key.T
+        key_t = keys_of(h).T
         value_t = value.T
         dk = jnp.zeros((4 * seg, DH), f32)
         dv = jnp.zeros((4 * seg, DH), f32)
-        groups = HQ // HK
         for pair in range(groups // 2):
-            at = (h * groups + 2 * pair) * DH
-            one, two = slice(at, at + DH), slice(at + DH, at + 2 * DH)
+            one, two = places(h, pair)
             q = jnp.concatenate([q_ref[:, one], q_ref[:, two]], axis=0)
             g = jnp.concatenate([g_ref[:, one], g_ref[:, two]], axis=0)
-            s = nt(key, q) * fold + bias[...]
-            e = jnp.exp2(s - jnp.max(s, axis=0, keepdims=True))
-            p = e * (1.0 / jnp.sum(e, axis=0, keepdims=True))
+            p = probs[h * (groups // 2) + pair]
             p_low = p.astype(bf16)
             dp = nt(value, g)
             delta = jnp.sum(p * dp, axis=0, keepdims=True)
@@ -278,58 +329,58 @@
             dq_ref[:, two] = dq[seg:]
             dk = dk + nn(ds, q)
             dv = dv + nn(p_low, g)
-            if pair == 1:
-                hook()
         for i in range(4):
-            terms[h, i, :, :DH] = (dk[i * seg : (i + 1) * seg] * scale).astype(bf16)
-            terms[h, i, :, DH:] = dv[i * seg : (i + 1) * seg].astype(bf16)
-
-    def term(h, target):
+            terms[h, i] = dv[i * seg : (i + 1) * seg].astype(bf16)
+            terms[HK + h, i] = (dk[i * seg : (i + 1) * seg] * scale).astype(bf16)
+
+    def term(m, target):
         slot = jnp.where(chain[0] == target, 0, jnp.where(chain[1] == target, 1, 2))
         hit = (chain[0] == target) | (chain[1] == target) | (chain[2] == target)
-        block = terms[h, slot]
+        block = terms[m, slot]
         return jnp.where(hit, block, jnp.zeros_like(block))
 
-    def x_copy(h, t):
-        return remote(x_out.at[h, t], x_in.at[h, t], gx_send.at[h, t], gx_recv.at[h, t], x_peer, grp)
-
-    def z_copy(h, t):
-        return remote(z_out.at[h, t], z_in.at[h, z], gz_send.at[h, t], gz_recv.at[h, z], t * NX + x, grp)
-
-    def x_stage(h):
+    def x_copy(m, t):
+        return remote(x_out.at[m, t], x_in.at[m, t], gx_send.at[m, t], gx_recv.at[m, t], x_peer, grp)
+
+    def z_copy(m, t):
+        return remote(z_out.at[m, t], z_in.at[m, z], gz_send.at[m, t], gz_recv.at[m, z], t * NX + x, grp)
+
+    def x_stage(m):
         for t in range(nz):
             @pl.when((t < z) | ((t == z) & (x == 1)))
             def _(t=t):
-                x_out[h, t] = term(h, t * NX + (1 - x))
-                x_copy(h, t).start()
-
-    def z_stage(h):
+                x_out[m, t] = term(m, t * NX + (1 - x))
+                x_copy(m, t).start()
+
+    def z_stage(m):
         for t in range(nz - 1):
             @pl.when(t < z)
             def _(t=t):
-                x_copy(h, t).wait_recv()
-                total = term(h, t * NX + x).astype(f32) + x_in[h, t].astype(f32)
-                z_out[h, t] = total.astype(bf16)
-                z_copy(h, t).start()
-
-    def owned(h):
-        acc[...] = terms[h, 3].astype(f32)
+                x_copy(m, t).wait_recv()
+                total = term(m, t * NX + x).astype(f32) + x_in[m, t].astype(f32)
+                z_out[m, t] = total.astype(bf16)
+                z_copy(m, t).start()
+
+    def owned(m):
+        acc[...] = terms[m, 3].astype(f32)
         for t in range(nz):
             @pl.when((t == z) & (x == 0))
             def _(t=t):
-                x_copy(h, t).wait_recv()
-                acc[...] += x_in[h, t].astype(f32)
+                x_copy(m, t).wait_recv()
+                acc[...] += x_in[m, t].astype(f32)
 
         for t in range(1, nz):
             @pl.when(t > z)
             def _(t=t):
-                block = z_in.at[h, t]
-                remote(block, block, gz_send.at[h, t], gz_recv.at[h, t], t * NX + x, grp).wait_recv()
-                acc[...] += z_in[h, t].astype(f32)
-
-        lanes = slice(h * DH, (h + 1) * DH)
-        dkey[:, lanes] = acc[:, :DH].astype(bf16)
-        dv_all[h // 2, grp, :, (h % 2) * DH : (h % 2 + 1) * DH] = acc[:, DH:].astype(bf16)
+                block = z_in.at[m, t]
+                remote(block, block, gz_send.at[m, t], gz_recv.at[m, t], t * NX + x, grp).wait_recv()
+                acc[...] += z_in[m, t].astype(f32)
+
+        h = m % HK
+        if m < HK:
+            dv_all[h // 2, grp, :, (h % 2) * DH : (h % 2 + 1) * DH] = acc[...].astype(bf16)
+        else:
+            dkey[:, h * DH : (h + 1) * DH] = acc[...].astype(bf16)
 
     def spread(part):
         mine = dv_all.at[part, grp]
@@ -341,8 +392,6 @@
         to_y.wait_recv()
         theirs = dv_all.at[part, y_peer]
         return start(remote(theirs, theirs, d_send.at[part, 2], d_recv.at[part, 2], leaf, c_peer))
-
-    rows = hidden_t.shape[3]
 
     def partials(part, side):
         total = nn(hidden_t[grp, side].reshape(nz * rows, seg), dv_all[part, grp])
@@ -377,41 +426,46 @@
             )
         return copies
 
-    head(0, lambda: forward(2))
-    x_stage(0)
-    head(1, lambda: forward(3))
-    x_stage(1)
-    z_stage(0)
-    head(2, lambda: None)
-    x_stage(2)
-    z_stage(1)
-    head(3, lambda: None)
-    x_stage(3)
-    z_stage(2)
+    for h in range(HK):
+        softmax(h)
+        forward(h)
+    for h in range(HK):
+        gradients(h)
+        x_stage(h)
+        if h > 0:
+            z_stage(h - 1)
+    z_stage(HK - 1)
+    for h in range(HK):
+        x_stage(HK + h)
     owned(0)
     owned(1)
     to_y, to_c = spread(0)
     for copy in hidden:
         copy.wait_recv()
-    z_stage(3)
     relayed = relay(0, to_y)
+    z_stage(HK)
     to_c.wait_recv()
     relayed.wait_recv()
     weight_x(0)
     owned(2)
     owned(3)
     to_y, to_c = spread(1)
+    z_stage(HK + 1)
+    relayed = relay(1, to_y)
+    z_stage(HK + 2)
+    to_c.wait_recv()
+    relayed.wait_recv()
+    weight_x(1)
+    z_stage(HK + 3)
+    copies = weight_z(0)
     width = hidden_ref.shape[1] // 4
     weight = w_all[...].reshape(hidden_ref.shape[1], w_ref.shape[1])
     dv_low = jnp.concatenate([dv_all[0, grp], dv_all[1, grp]], axis=1)
-    copies = weight_z(0)
-    relayed = relay(1, to_y)
-    to_c.wait_recv()
-    relayed.wait_recv()
-    weight_x(1)
     for i in range(4):
         dhidden[:, i * width : (i + 1) * width] = nt(dv_low, weight[i * width : (i + 1) * width, :]).astype(bf16)
     copies += weight_z(1)
+    for h in range(HK):
+        owned(HK + h)
     for copy in copies:
         copy.wait_recv()
     for part in range(2):
@@ -424,14 +478,15 @@
     for h in range(HK):
         up, across = v_sems(h)
         sent(values[h].at[leaf], values[h], up, across)
+    for m in range(2 * HK):
         for t in range(nz):
             @pl.when((t < z) | ((t == z) & (x == 1)))
-            def _(t=t, h=h):
-                x_copy(h, t).wait_send()
+            def _(t=t, m=m):
+                x_copy(m, t).wait_send()
         for t in range(nz - 1):
             @pl.when(t < z)
-            def _(t=t, h=h):
-                z_copy(h, t).wait_send()
+            def _(t=t, m=m):
+                z_copy(m, t).wait_send()
     for copy in pending:
         copy.wait_send()
 
@@ -443,7 +498,6 @@
     nz, ny = n_leaf // NX, n_grp // NC
     half = width // 2
     bf16, f32 = jnp.bfloat16, jnp.float32
-    hidden_t = hidden.T.reshape(nz, NX, n_grp, rows, seg).transpose(2, 1, 0, 3, 4)
     vmem = pl.BlockSpec(memory_space=pltpu.VMEM)
     anywhere = pl.BlockSpec(memory_space=pl.ANY)
     held, dma = pltpu.VMEM, pltpu.SemaphoreType.DMA
@@ -457,11 +511,12 @@
             jax.ShapeDtypeStruct(hidden.shape, bf16),
             jax.ShapeDtypeStruct(value_weight.shape, f32),
         ],
-        in_specs=[pl.BlockSpec(memory_space=pltpu.SMEM)] + [vmem] * 4 + [anywhere] * 2,
+        in_specs=[pl.BlockSpec(memory_space=pltpu.SMEM)] + [vmem] * 3 + [anywhere] * 2,
         out_specs=[vmem] * 5,
         scratch_shapes=[
             held(q.shape, bf16),
             held(q.shape, bf16),
+            held((n_grp, NX, nz, rows, seg), bf16),
             held((nz, NX, ny, NC, rows, width), bf16),
             held((n_leaf, seg, width), bf16),
         ]
@@ -471,11 +526,12 @@
             held((8, 128), jnp.int32),
             pltpu.SMEM((n_leaf, 128), jnp.int32),
             held((4 * seg, 2 * seg), f32),
-            held((HK, 4, seg, 2 * DH), bf16),
+            held((HQ // 2, 4 * seg, 2 * seg), f32),
+            held((2 * HK, 4, seg, DH), bf16),
         ]
-        + [held((HK, nz, seg, 2 * DH), bf16)] * 4
+        + [held((2 * HK, nz, seg, DH), bf16)] * 4
         + [
-            held((seg, 2 * DH), f32),
+            held((seg, DH), f32),
             held((n_grp, NX, nz, rows, seg), bf16),
             held((2, n_grp, seg, half), bf16),
             held((2, nz, rows, half), bf16),
@@ -485,14 +541,14 @@
             dma((3,)),
         ]
         + pairs(n_leaf - 1)
-        + pairs(nz - 1)
-        + pairs(4)
-        + pairs(5)
+        + pairs(2, nz - 1)
+        + pairs(2, 4)
+        + pairs(2, 5)
         + pairs(nz - 1)
         + pairs(nz)
         + pairs(HK, nz - 1)
         + pairs(HK, nz)
-        + pairs(HK, nz) * 2
+        + pairs(2 * HK, nz) * 2
         + pairs(n_grp - 1)
         + pairs(2, 3)
         + pairs(2)
@@ -505,7 +561,7 @@
             bytes_accessed=10000000,
             transcendentals=HQ * seg * 4 * seg,
         ),
-    )(parent_links, value_weight, key, hidden, hidden_t, q, g)
+    )(parent_links, value_weight, key, hidden, q, g)
     return out[None], dq[None], dkey[None], dhidden[None], dweight
 
 

time: 104 us -> 98 us (0.942)
  Pallas kernels: 94.8 us -> 90.7 us
  local copies, waits for them, and re-layouts: 8.09 us -> 5.79 us
    pallas_call x1, Pallas kernels: 94.8 us -> 90.7 us  [fast_shards(): pl.pallas_call(functools.partial(tree_kernel, n_leaf, n_grp), out_shape=[...]
    transpose x1 -> x0, local copies, waits for them, and re-layouts: 1.41 us -> none  [fast_shards(): hidden.T.reshape(nz, NX, n_grp, rows, seg).transpose(2, 1, 0, 3, 4)]
where the time goes in v3:
time: 98 us; the launch traced here: 97.8 us
  Pallas kernels  90.7 us (93%)
  local copies, waits for them, and re-layouts  5.79 us (6%)
  between operations  1.3 us (1%)
    pallas_call x1, Pallas kernels, fast_shards(): pl.pallas_call(functools.partial(tree_kernel, n_leaf, n_grp), out_shape=[...  90.7 us
    unnamed x13, local copies, waits for them, and re-layouts  5.79 us

profile of v3, /device:TPU:0, one launch (start us, length us, event | category | flops | bytes accessed | tf_op | source)
XLA Modules:
  0.0 97.8 jit_solution(18375715267963623193)
XLA Ops:
  1.3 90.7 %shard_map.101 = (bf16[128,5120]{1,0:T(8,128)(2,1)}, bf16[128,5120]{1,0:T(8,128)(2,1)}, bf16[128,512]{1,0:T(8,128)(2,1)}, bf16[128,2560]{1,0:T(8,128)(2,1)}, f32[80,512]{1,0:T(8,128)}) custom-call(s32[1,1]{1,0:T(1,128)S(6)} %copy.16.parent_ref, bf16[80,512]{1,0:T(8,128)(2,1)} %w_ref.1, bf16[128,512]{1,0:T(8,128)(2,1)} %bitcast.15, ...), custom_call_target="tpu_custom_call" | custom-call | flops 5033164800 | bytes 10000000 | tf_op jit(solution)/shard_map/pallas_call | solution.py:505
  92.0 0.0 copy-start
  92.0 2.6 %copy.17 = bf16[1,128,5120]{2,1,0:T(8,128)(2,1)} copy(bf16[1,128,5120]{2,1,0:T(8,128)(2,1)} %bitcast.9) | data formatting | bytes 2621440
  94.6 0.0 copy-done
  94.6 0.0 copy-start.3
  94.6 0.0 copy-start.1
  94.6 1.1 %copy.18 = bf16[1,128,5120]{2,1,0:T(8,128)(2,1)} copy(bf16[1,128,5120]{2,1,0:T(8,128)(2,1)S(1)} %bitcast.8) | data formatting | bytes 2621440
  95.6 0.0 copy-done.3
  95.7 0.0 copy-start.2
  95.7 0.7 copy.19
  96.3 0.0 copy-done.1
  96.3 0.8 copy.20
  97.1 0.0 copy-done.2
  97.2 0.7 copy.21
Async XLA Ops:
  92.0 2.6 %copy-start = (bf16[128,5120]{1,0:T(8,128)(2,1)S(1)}, bf16[128,5120]{1,0:T(8,128)(2,1)}, u32[]{:S(2)}) copy-start(bf16[128,5120]{1,0:T(8,128)(2,1)} %get-tuple-element.11) | copy-start | bytes 3932164
  94.6 1.1 %copy-start.3 = (bf16[128,512]{1,0:T(8,128)(2,1)S(1)}, bf16[128,512]{1,0:T(8,128)(2,1)}, u32[]{:S(2)}) copy-start(bf16[128,512]{1,0:T(8,128)(2,1)} %get-tuple-element.12) | copy-start | bytes 393220
  94.6 1.7 %copy-start.1 = (bf16[128,2560]{1,0:T(8,128)(2,1)S(1)}, bf16[128,2560]{1,0:T(8,128)(2,1)}, u32[]{:S(2)}) copy-start(bf16[128,2560]{1,0:T(8,128)(2,1)} %get-tuple-element.13) | copy-start | bytes 1966084
  95.7 1.5 %copy-start.2 = (f32[80,512]{1,0:T(8,128)S(1)}, f32[80,512]{1,0:T(8,128)}, u32[]{:S(2)}) copy-start(f32[80,512]{1,0:T(8,128)} %get-tuple-element.24) | copy-start | bytes 491524

commit v4 on v3

--- a/solution.py
+++ b/solution.py
@@ -64,10 +64,10 @@
 def tree_kernel(
     n_leaf, n_grp,
     parent_ref, w_ref, key_ref, hidden_ref, q_hbm, g_hbm,
-    out_ref, dq_ref, dkey, dhidden, dweight,
-    q_ref, g_ref, hidden_t, w_all, key_all, v0, v1, v2, v3, parents, own_parent, par, bias, probs, terms,
+    out_hbm, dq_hbm, dkey, dhidden, dweight,
+    q_ref, g_ref, out_ref, dq_ref, hidden_t, w_all, k0, k1, k2, k3, v0, v1, v2, v3, parents, own_parent, par, bias, probs, terms,
     x_out, x_in, z_out, z_in, acc, hid_all, dv_all, px_out, px_in, pz_out, pz_in,
-    load_sem, par_send, par_recv, wz_send, wz_recv, w_send, w_recv, c_send, c_recv,
+    load_sem, store_sem, par_send, par_recv, wz_send, wz_recv, w_send, w_recv, c_send, c_recv,
     kz_send, kz_recv, kx_send, kx_recv, vz_send, vz_recv, vx_send, vx_recv,
     gx_send, gx_recv, gz_send, gz_recv, h_send, h_recv, d_send, d_recv,
     px_send, px_recv, pz_send, pz_recv,
@@ -79,7 +79,7 @@
     scale = 1.0 / DH**0.5
     fold = scale * 1.4426950408889634
     x_peer, y_peer, c_peer = z * NX + (1 - x), (1 - y) * NC + c, y * NC + (1 - c)
-    values = (v0, v1, v2, v3)
+    keys, values = (k0, k1, k2, k3), (v0, v1, v2, v3)
     half = w_ref.shape[1] // 2
     pending = []
 
@@ -98,19 +98,22 @@
         return copy
 
     def w_over_z(part):
-        lanes = pl.ds(part * half, half)
         copies = []
+        two = pl.ds(2 * part, 2)
         for d in range(1, nz):
             copies.append(
                 start(
                     remote(
-                        w_ref.at[:, lanes], w_all.at[z, x, y, c, :, lanes],
+                        w_all.at[two, z, x, y, c], w_all.at[two, z, x, y, c],
                         wz_send.at[part, d - 1], wz_recv.at[part, d - 1], lax.rem(z + d, nz) * NX + x, grp,
                     )
                 )
             )
         return copies
 
+    quarter = half // 2
+    for i in range(4):
+        w_all[i, z, x, y, c] = w_ref[:, i * quarter : (i + 1) * quarter]
     wz = w_over_z(0)
     links = []
     for d in range(1, n_leaf):
@@ -118,8 +121,8 @@
         links.append(
             start(remote(own_parent, parents.at[leaf], par_send.at[d - 1], par_recv.at[d - 1], to, grp))
         )
-    w_all[z, x, y, c] = w_ref[...]
-    key_all[leaf] = key_ref[...]
+    for h in range(HK):
+        keys[h][leaf] = key_ref[:, h * DH : (h + 1) * DH]
     parents[leaf] = own_parent[...]
 
     def up_copy(block, whole, sems, d):
@@ -173,7 +176,13 @@
         def _():
             remote(block, whole.at[leaf], sems[0].at[0], sems[1].at[0], x_peer, grp).wait_send()
 
-    k_up, k_across = (kz_send, kz_recv), (kx_send, kx_recv)
+    def k_sems(h):
+        return (kz_send.at[h], kz_recv.at[h]), (kx_send.at[h], kx_recv.at[h])
+
+    def k_forward(h):
+        up, across = k_sems(h)
+        across_own(keys[h].at[leaf], keys[h], across)
+        across_start(keys[h], up, across)
 
     rows = hidden_t.shape[3]
     for first in range(nz):
@@ -184,11 +193,7 @@
                 at = (i * n_grp + j) * rows
                 hidden_t[j, i, first] = turned[at : at + rows]
 
-    quarter = half // 2
     to_core = [[], []]
-
-    def lanes_of(part):
-        return pl.ds(part * half, quarter), pl.ds(part * half + quarter, quarter)
 
     def w_copy(part, i, block, leaf_to, grp_to):
         return start(remote(block, block, w_send.at[part, i], w_recv.at[part, i], leaf_to, grp_to))
@@ -199,29 +204,29 @@
         )
 
     def w_first(part):
-        a, b = lanes_of(part)
+        a, b = 2 * part, 2 * part + 1
         return (
-            w_copy(part, 0, w_all.at[:, x, y, c, :, a], x_peer, grp),
-            w_copy(part, 1, w_all.at[:, x, y, c, :, b], leaf, y_peer),
+            w_copy(part, 0, w_all.at[a, :, x, y, c], x_peer, grp),
+            w_copy(part, 1, w_all.at[b, :, x, y, c], leaf, y_peer),
         )
 
     def w_second(part, first):
-        a, b = lanes_of(part)
+        a, b = 2 * part, 2 * part + 1
         first[0].wait_recv()
-        over_y = w_copy(part, 2, w_all.at[:, :, y, c, :, a], leaf, y_peer)
+        over_y = w_copy(part, 2, w_all.at[a, :, :, y, c], leaf, y_peer)
         first[1].wait_recv()
-        over_x = w_copy(part, 3, w_all.at[:, x, :, c, :, b], x_peer, grp)
-        w_core(part, 0, w_all.at[:, x, y, c, :, pl.ds(part * half, half)])
-        w_core(part, 1, w_all.at[:, 1 - x, y, c, :, a])
-        w_core(part, 2, w_all.at[:, x, 1 - y, c, :, b])
+        over_x = w_copy(part, 3, w_all.at[b, :, x, :, c], x_peer, grp)
+        w_core(part, 0, w_all.at[pl.ds(2 * part, 2), :, x, y, c])
+        w_core(part, 1, w_all.at[a, :, 1 - x, y, c])
+        w_core(part, 2, w_all.at[b, :, x, 1 - y, c])
         return over_y, over_x
 
     def w_third(part, second):
-        a, b = lanes_of(part)
+        a, b = 2 * part, 2 * part + 1
         second[0].wait_recv()
-        w_core(part, 3, w_all.at[:, :, 1 - y, c, :, a])
+        w_core(part, 3, w_all.at[a, :, :, 1 - y, c])
         second[1].wait_recv()
-        w_core(part, 4, w_all.at[:, 1 - x, :, c, :, b])
+        w_core(part, 4, w_all.at[b, :, 1 - x, :, c])
 
     def v_sems(h):
         return (vz_send.at[h], vz_recv.at[h]), (vx_send.at[h], vx_recv.at[h])
@@ -229,7 +234,9 @@
     def project(part):
         for copy in to_core[part]:
             copy.wait_recv()
-        weight = w_all[:, :, :, :, :, part * half : (part + 1) * half].reshape(hidden_ref.shape[1], half)
+        weight = jnp.concatenate(
+            [w_all[2 * part + i].reshape(hidden_ref.shape[1], quarter) for i in range(2)], axis=1
+        )
         pair = nn(hidden_ref[...], weight).astype(bf16)
         for i in range(HK // 2):
             h = part * (HK // 2) + i
@@ -247,13 +254,14 @@
     for copy in wz:
         copy.wait_recv()
     first1 = w_first(1)
-    up_start(key_ref, key_all, k_up)
+    for h in range(HK):
+        up_start(keys[h].at[leaf], keys[h], k_sems(h)[0])
     w_third(0, second0)
     second1 = w_second(1, first1)
     project(0)
+    k_forward(0)
     w_third(1, second1)
-    across_own(key_ref, key_all, k_across)
-    across_start(key_all, k_up, k_across)
+    k_forward(1)
     hidden = []
     for d in range(1, n_grp):
         to = lax.rem(grp + d, n_grp)
@@ -261,6 +269,8 @@
             start(remote(hidden_t.at[to], hid_all.at[d], h_send.at[d - 1], h_recv.at[d - 1], leaf, to))
         )
     project(1)
+    k_forward(2)
+    k_forward(3)
     for copy in links:
         copy.wait_recv()
     listing = pltpu.make_async_copy(parents.at[:, 0], par, load_sem.at[2])
@@ -281,7 +291,6 @@
     row = lax.broadcasted_iota(jnp.int32, (seg, 2 * seg), 1)
     row = jnp.where(row >= seg, row - seg, row)
     bias[3 * seg :, :] = jnp.where(col <= row, 0.0, -1e30)
-    across_ready(key_ref, key_all, k_across)
     for load in loads:
         load.wait()
 
@@ -293,9 +302,10 @@
         return slice(at, at + DH), slice(at + DH, at + 2 * DH)
 
     def keys_of(h):
-        return jnp.concatenate([key_all[slot, :, h * DH : (h + 1) * DH] for slot in slots], axis=0)
+        return jnp.concatenate([keys[h][slot] for slot in slots], axis=0)
 
     def softmax(h):
+        across_ready(keys[h].at[leaf], keys[h], k_sems(h)[1])
         key = keys_of(h)
         for pair in range(groups // 2):
             one, two = places(h, pair)
@@ -303,6 +313,13 @@
             s = nt(key, q) * fold + bias[...]
             e = jnp.exp2(s - jnp.max(s, axis=0, keepdims=True))
             probs[h * (groups // 2) + pair] = e * (1.0 / jnp.sum(e, axis=0, keepdims=True))
+
+    def stores(h):
+        lanes = pl.ds(h * groups * DH, groups * DH)
+        return (
+            pltpu.make_async_copy(out_ref.at[:, lanes], out_hbm.at[:, lanes], store_sem.at[h, 0]),
+            pltpu.make_async_copy(dq_ref.at[:, lanes], dq_hbm.at[:, lanes], store_sem.at[h, 1]),
+        )
 
     def gradients(h):
         up, across = v_sems(h)
@@ -329,6 +346,8 @@
             dq_ref[:, two] = dq[seg:]
             dk = dk + nn(ds, q)
             dv = dv + nn(p_low, g)
+        for store in stores(h):
+            store.start()
         for i in range(4):
             terms[h, i] = dv[i * seg : (i + 1) * seg].astype(bf16)
             terms[HK + h, i] = (dk[i * seg : (i + 1) * seg] * scale).astype(bf16)
@@ -459,7 +478,7 @@
     z_stage(HK + 3)
     copies = weight_z(0)
     width = hidden_ref.shape[1] // 4
-    weight = w_all[...].reshape(hidden_ref.shape[1], w_ref.shape[1])
+    weight = jnp.concatenate([w_all[i].reshape(hidden_ref.shape[1], quarter) for i in range(4)], axis=1)
     dv_low = jnp.concatenate([dv_all[0, grp], dv_all[1, grp]], axis=1)
     for i in range(4):
         dhidden[:, i * width : (i + 1) * width] = nt(dv_low, weight[i * width : (i + 1) * width, :]).astype(bf16)
@@ -474,8 +493,9 @@
             total = total + pz_in[part, 1, d - 1].astype(f32)
         dweight[:, part * half : (part + 1) * half] = total
 
-    sent(key_ref, key_all, k_up, k_across)
     for h in range(HK):
+        up, across = k_sems(h)
+        sent(keys[h].at[leaf], keys[h], up, across)
         up, across = v_sems(h)
         sent(values[h].at[leaf], values[h], up, across)
     for m in range(2 * HK):
@@ -489,6 +509,36 @@
                 z_copy(m, t).wait_send()
     for copy in pending:
         copy.wait_send()
+    for h in range(HK):
+        for store in stores(h):
+            store.wait()
+
+
+def hand_over_kernel(*refs):
+    sems = refs[10]
+    copies = [pltpu.make_async_copy(refs[i], refs[5 + i], sems.at[i]) for i in range(2, 5)]
+    half = refs[0].shape[0] // 2
+    for i in range(2):
+        for j in range(2):
+            rows = pl.ds(j * half, half)
+            sem = sems.at[i if j == 0 else 5 + i]
+            copies.append(pltpu.make_async_copy(refs[i].at[rows], refs[5 + i].at[rows], sem))
+    for copy in copies:
+        copy.start()
+    for copy in copies:
+        copy.wait()
+
+
+def hand_over(*arrays):
+    anywhere = pl.BlockSpec(memory_space=pl.ANY)
+    return pl.pallas_call(
+        hand_over_kernel,
+        out_shape=[jax.ShapeDtypeStruct(a.shape, a.dtype) for a in arrays],
+        in_specs=[anywhere] * 5,
+        out_specs=[anywhere] * 5,
+        scratch_shapes=[pltpu.SemaphoreType.DMA((7,))],
+        compiler_params=pltpu.CompilerParams(vmem_limit_bytes=VMEM_LIMIT),
+    )(*arrays)
 
 
 def fast_shards(n_leaf, n_grp, hidden_states, query_rows, key_rows, value_weight, parent_links, out_grad):
@@ -512,15 +562,16 @@
             jax.ShapeDtypeStruct(value_weight.shape, f32),
         ],
         in_specs=[pl.BlockSpec(memory_space=pltpu.SMEM)] + [vmem] * 3 + [anywhere] * 2,
-        out_specs=[vmem] * 5,
+        out_specs=[anywhere] * 2 + [vmem] * 3,
         scratch_shapes=[
             held(q.shape, bf16),
             held(q.shape, bf16),
+            held(q.shape, bf16),
+            held(q.shape, bf16),
             held((n_grp, NX, nz, rows, seg), bf16),
-            held((nz, NX, ny, NC, rows, width), bf16),
-            held((n_leaf, seg, width), bf16),
+            held((4, nz, NX, ny, NC, rows, width // 4), bf16),
         ]
-        + [held((n_leaf, seg, DH), bf16)] * HK
+        + [held((n_leaf, seg, DH), bf16)] * (2 * HK)
         + [
             held((n_leaf, 8, 128), jnp.int32),
             held((8, 128), jnp.int32),
@@ -539,13 +590,14 @@
             held((2, nz, rows, half), f32),
             held((2, 2, nz - 1, rows, half), bf16),
             dma((3,)),
+            dma((HK, 2)),
         ]
         + pairs(n_leaf - 1)
         + pairs(2, nz - 1)
         + pairs(2, 4)
         + pairs(2, 5)
-        + pairs(nz - 1)
-        + pairs(nz)
+        + pairs(HK, nz - 1)
+        + pairs(HK, nz)
         + pairs(HK, nz - 1)
         + pairs(HK, nz)
         + pairs(2 * HK, nz) * 2
@@ -562,6 +614,7 @@
             transcendentals=HQ * seg * 4 * seg,
         ),
     )(parent_links, value_weight, key, hidden, q, g)
+    out, dq, dkey, dhidden, dweight = hand_over(out, dq, dkey, dhidden, dweight)
     return out[None], dq[None], dkey[None], dhidden[None], dweight
 
 

time: 98 us -> 201 us (2.05)
  Pallas kernels: 90.7 us -> 199 us
  local copies, waits for them, and re-layouts: 5.79 us -> 0 us
    pallas_call x0 -> x1, Pallas kernels: none -> 109 us  [hand_over(): pl.pallas_call(hand_over_kernel, out_shape=[jax.ShapeDtypeStruct(a.shape,...]
    unnamed x13 -> x0, local copies, waits for them, and re-layouts: 5.79 us -> none
where the time goes in v4:
time: 201 us
  Pallas kernels  199 us (99%)
    pallas_call x1, Pallas kernels, hand_over(): pl.pallas_call(hand_over_kernel, out_shape=[jax.ShapeDtypeStruct(a.shape,...  109 us
    pallas_call x1, Pallas kernels, fast_shards(): pl.pallas_call(functools.partial(tree_kernel, n_leaf, n_grp), out_shape=[...  89.8 us

profile of v4, /device:TPU:0, one launch (start us, length us, event | category | flops | bytes accessed | tf_op | source)
XLA Modules:
  0.0 200.6 jit_solution(6717657625049773856)
XLA Ops:
  1.3 89.8 %shard_map.101 = (bf16[128,5120]{1,0:T(8,128)(2,1)}, bf16[128,5120]{1,0:T(8,128)(2,1)}, bf16[128,512]{1,0:T(8,128)(2,1)}, bf16[128,2560]{1,0:T(8,128)(2,1)}, f32[80,512]{1,0:T(8,128)}) custom-call(s32[1,1]{1,0:T(1,128)S(6)} %copy.11.parent_ref, bf16[80,512]{1,0:T(8,128)(2,1)} %w_ref.1, bf16[128,512]{1,0:T(8,128)(2,1)} %bitcast.14, ...), custom_call_target="tpu_custom_call" | custom-call | flops 5033164800 | bytes 10000000 | tf_op jit(solution)/shard_map/pallas_call | solution.py:555
  91.1 109.4 %shard_map.102 = (bf16[128,5120]{1,0:T(8,128)(2,1)}, bf16[128,5120]{1,0:T(8,128)(2,1)}, bf16[128,512]{1,0:T(8,128)(2,1)}, bf16[128,2560]{1,0:T(8,128)(2,1)}, f32[80,512]{1,0:T(8,128)}) custom-call(bf16[128,5120]{1,0:T(8,128)(2,1)} %get-tuple-element.15.refs_0_, bf16[128,5120]{1,0:T(8,128)(2,1)} %get-tuple-element.16.refs_1_, ...), custom_call_target="tpu_custom_call" | custom-call | tf_op jit(solution)/shard_map/pallas_call | solution.py:534

commit v5 on v4

--- a/solution.py
+++ b/solution.py
@@ -65,7 +65,7 @@
     n_leaf, n_grp,
     parent_ref, w_ref, key_ref, hidden_ref, q_hbm, g_hbm,
     out_hbm, dq_hbm, dkey, dhidden, dweight,
-    q_ref, g_ref, out_ref, dq_ref, hidden_t, w_all, k0, k1, k2, k3, v0, v1, v2, v3, parents, own_parent, par, bias, probs, terms,
+    q_ref, g_ref, out_ref, dq_ref, hidden_t, w_all, k0, k1, v0, v1, parents, own_parent, par, bias, probs, terms,
     x_out, x_in, z_out, z_in, acc, hid_all, dv_all, px_out, px_in, pz_out, pz_in,
     load_sem, store_sem, par_send, par_recv, wz_send, wz_recv, w_send, w_recv, c_send, c_recv,
     kz_send, kz_recv, kx_send, kx_recv, vz_send, vz_recv, vx_send, vx_recv,
@@ -79,8 +79,9 @@
     scale = 1.0 / DH**0.5
     fold = scale * 1.4426950408889634
     x_peer, y_peer, c_peer = z * NX + (1 - x), (1 - y) * NC + c, y * NC + (1 - c)
-    keys, values = (k0, k1, k2, k3), (v0, v1, v2, v3)
+    keys, values = (k0, k1), (v0, v1)
     half = w_ref.shape[1] // 2
+    spot = x * nz + z
     pending = []
 
     loads = [
@@ -121,68 +122,55 @@
         links.append(
             start(remote(own_parent, parents.at[leaf], par_send.at[d - 1], par_recv.at[d - 1], to, grp))
         )
-    for h in range(HK):
-        keys[h][leaf] = key_ref[:, h * DH : (h + 1) * DH]
+    for part in range(2):
+        keys[part][spot] = key_ref[:, part * half : (part + 1) * half]
     parents[leaf] = own_parent[...]
 
-    def up_copy(block, whole, sems, d):
-        return remote(block, whole.at[leaf], sems[0].at[d - 1], sems[1].at[d - 1], leaf + d * NX, grp)
-
-    def up_start(block, whole, sems):
+    def up_copy(whole, sems, part, d):
+        block = whole[part].at[spot]
+        return remote(block, block, sems[0].at[part, d - 1], sems[1].at[part, d - 1], leaf + d * NX, grp)
+
+    def up_start(whole, sems, part):
         for d in range(1, nz):
             @pl.when(z + d < nz)
             def _(d=d):
-                up_copy(block, whole, sems, d).start()
-
-    def across_own(block, whole, sems):
-        @pl.when(x == 0)
-        def _():
-            remote(block, whole.at[leaf], sems[0].at[0], sems[1].at[0], x_peer, grp).start()
-
-    def across_copy(whole, sems, d):
-        slot = leaf - d * NX
-        return remote(whole.at[slot], whole.at[slot], sems[0].at[d], sems[1].at[d], x_peer, grp)
-
-    def across_start(whole, up_sems, sems):
+                up_copy(whole, sems, part, d).start()
+
+    def across_copy(whole, sems, part, k, column):
+        blocks = whole[part].at[pl.ds(column * nz, k + 1)]
+        return remote(blocks, blocks, sems[2].at[part], sems[3].at[part], x_peer, grp)
+
+    def across_start(whole, sems, part):
         for d in range(1, nz):
             @pl.when(z - d >= 0)
             def _(d=d):
-                slot = leaf - d * NX
-                remote(whole.at[slot], whole.at[slot], up_sems[0].at[d - 1], up_sems[1].at[d - 1], leaf, grp).wait_recv()
-                across_copy(whole, sems, d).start()
-
-    def across_ready(block, whole, sems):
-        for d in range(1, nz):
-            @pl.when(z - d >= 0)
-            def _(d=d):
-                slot = x_peer - d * NX
-                remote(whole.at[slot], whole.at[slot], sems[0].at[d], sems[1].at[d], x_peer, grp).wait_recv()
-
-        @pl.when(x == 1)
-        def _():
-            remote(block, whole.at[x_peer], sems[0].at[0], sems[1].at[0], x_peer, grp).wait_recv()
-
-    def sent(block, whole, up_sems, sems):
+                block = whole[part].at[spot - d]
+                remote(block, block, sems[0].at[part, d - 1], sems[1].at[part, d - 1], leaf, grp).wait_recv()
+
+        for k in range(nz):
+            @pl.when(z == k)
+            def _(k=k):
+                across_copy(whole, sems, part, k, x).start()
+
+    def across_ready(whole, sems, part):
+        for k in range(nz):
+            @pl.when(z == k)
+            def _(k=k):
+                across_copy(whole, sems, part, k, 1 - x).wait_recv()
+
+    def sent(whole, sems, part):
         for d in range(1, nz):
             @pl.when(z + d < nz)
             def _(d=d):
-                up_copy(block, whole, up_sems, d).wait_send()
-
-            @pl.when(z - d >= 0)
-            def _(d=d):
-                across_copy(whole, sems, d).wait_send()
-
-        @pl.when(x == 0)
-        def _():
-            remote(block, whole.at[leaf], sems[0].at[0], sems[1].at[0], x_peer, grp).wait_send()
-
-    def k_sems(h):
-        return (kz_send.at[h], kz_recv.at[h]), (kx_send.at[h], kx_recv.at[h])
-
-    def k_forward(h):
-        up, across = k_sems(h)
-        across_own(keys[h].at[leaf], keys[h], across)
-        across_start(keys[h], up, across)
+                up_copy(whole, sems, part, d).wait_send()
+
+        for k in range(nz):
+            @pl.when(z == k)
+            def _(k=k):
+                across_copy(whole, sems, part, k, x).wait_send()
+
+    k_sems = (kz_send, kz_recv, kx_send, kx_recv)
+    v_sems = (vz_send, vz_recv, vx_send, vx_recv)
 
     rows = hidden_t.shape[3]
     for first in range(nz):
@@ -228,9 +216,6 @@
         second[1].wait_recv()
         w_core(part, 4, w_all.at[b, :, 1 - x, :, c])
 
-    def v_sems(h):
-        return (vz_send.at[h], vz_recv.at[h]), (vx_send.at[h], vx_recv.at[h])
-
     def project(part):
         for copy in to_core[part]:
             copy.wait_recv()
@@ -238,13 +223,8 @@
             [w_all[2 * part + i].reshape(hidden_ref.shape[1], quarter) for i in range(2)], axis=1
         )
         pair = nn(hidden_ref[...], weight).astype(bf16)
-        for i in range(HK // 2):
-            h = part * (HK // 2) + i
-            whole = values[h]
-            whole[leaf] = pair[:, i * DH : (i + 1) * DH]
-            up, across = v_sems(h)
-            up_start(whole.at[leaf], whole, up)
-            across_own(whole.at[leaf], whole, across)
+        values[part][spot] = pair
+        up_start(values, v_sems, part)
 
     for copy in wz:
         copy.wait_recv()
@@ -254,14 +234,13 @@
     for copy in wz:
         copy.wait_recv()
     first1 = w_first(1)
-    for h in range(HK):
-        up_start(keys[h].at[leaf], keys[h], k_sems(h)[0])
+    for part in range(2):
+        up_start(keys, k_sems, part)
     w_third(0, second0)
     second1 = w_second(1, first1)
     project(0)
-    k_forward(0)
+    across_start(keys, k_sems, 0)
     w_third(1, second1)
-    k_forward(1)
     hidden = []
     for d in range(1, n_grp):
         to = lax.rem(grp + d, n_grp)
@@ -269,17 +248,11 @@
             start(remote(hidden_t.at[to], hid_all.at[d], h_send.at[d - 1], h_recv.at[d - 1], leaf, to))
         )
     project(1)
-    k_forward(2)
-    k_forward(3)
+    across_start(keys, k_sems, 1)
     for copy in links:
         copy.wait_recv()
     listing = pltpu.make_async_copy(parents.at[:, 0], par, load_sem.at[2])
     listing.start()
-
-    def forward(h):
-        if h < HK:
-            up, across = v_sems(h)
-            across_start(values[h], up, across)
 
     listing.wait()
     chain = ancestors_of(par, leaf)
@@ -295,17 +268,22 @@
         load.wait()
 
     groups = HQ // HK
-    slots = [jnp.maximum(chain[i], 0) for i in range(3)] + [leaf]
+    above = [jnp.maximum(chain[i], 0) for i in range(3)]
+    slots = [lax.rem(a, NX) * nz + lax.div(a, NX) for a in above] + [spot]
+
+    def lanes_in(h):
+        return slice(h % 2 * DH, (h % 2 + 1) * DH)
 
     def places(h, pair):
         at = (h * groups + 2 * pair) * DH
         return slice(at, at + DH), slice(at + DH, at + 2 * DH)
 
     def keys_of(h):
-        return jnp.concatenate([keys[h][slot] for slot in slots], axis=0)
+        return jnp.concatenate([keys[h // 2][slot, :, lanes_in(h)] for slot in slots], axis=0)
 
     def softmax(h):
-        across_ready(keys[h].at[leaf], keys[h], k_sems(h)[1])
+        if h % 2 == 0:
+            across_ready(keys, k_sems, h // 2)
         key = keys_of(h)
         for pair in range(groups // 2):
             one, two = places(h, pair)
@@ -322,9 +300,9 @@
         )
 
     def gradients(h):
-        up, across = v_sems(h)
-        across_ready(values[h].at[leaf], values[h], across)
-        value = jnp.concatenate([values[h][slot] for slot in slots], axis=0)
+        if h % 2 == 0:
+            across_ready(values, v_sems, h // 2)
+        value = jnp.concatenate([values[h // 2][slot, :, lanes_in(h)] for slot in slots], axis=0)
         key_t = keys_of(h).T
         value_t = value.T
         dk = jnp.zeros((4 * seg, DH), f32)
@@ -349,8 +327,8 @@
         for store in stores(h):
             store.start()
         for i in range(4):
-            terms[h, i] = dv[i * seg : (i + 1) * seg].astype(bf16)
-            terms[HK + h, i] = (dk[i * seg : (i + 1) * seg] * scale).astype(bf16)
+            terms[h // 2, i, :, lanes_in(h)] = dv[i * seg : (i + 1) * seg].astype(bf16)
+            terms[2 + h // 2, i, :, lanes_in(h)] = (dk[i * seg : (i + 1) * seg] * scale).astype(bf16)
 
     def term(m, target):
         slot = jnp.where(chain[0] == target, 0, jnp.where(chain[1] == target, 1, 2))
@@ -358,36 +336,33 @@
         block = terms[m, slot]
         return jnp.where(hit, block, jnp.zeros_like(block))
 
-    def x_copy(m, t):
-        return remote(x_out.at[m, t], x_in.at[m, t], gx_send.at[m, t], gx_recv.at[m, t], x_peer, grp)
+    def x_copy(m, k):
+        blocks = pl.ds(0, k + 1)
+        return remote(x_out.at[m, blocks], x_in.at[m, blocks], gx_send.at[m], gx_recv.at[m], x_peer, grp)
 
     def z_copy(m, t):
         return remote(z_out.at[m, t], z_in.at[m, z], gz_send.at[m, t], gz_recv.at[m, z], t * NX + x, grp)
 
     def x_stage(m):
-        for t in range(nz):
-            @pl.when((t < z) | ((t == z) & (x == 1)))
-            def _(t=t):
-                x_out[m, t] = term(m, t * NX + (1 - x))
-                x_copy(m, t).start()
+        for k in range(nz):
+            @pl.when(z == k)
+            def _(k=k):
+                for t in range(k + 1):
+                    x_out[m, t] = term(m, t * NX + (1 - x))
+                x_copy(m, k).start()
 
     def z_stage(m):
-        for t in range(nz - 1):
-            @pl.when(t < z)
-            def _(t=t):
-                x_copy(m, t).wait_recv()
-                total = term(m, t * NX + x).astype(f32) + x_in[m, t].astype(f32)
-                z_out[m, t] = total.astype(bf16)
-                z_copy(m, t).start()
+        for k in range(nz):
+            @pl.when(z == k)
+            def _(k=k):
+                x_copy(m, k).wait_recv()
+                for t in range(k):
+                    total = term(m, t * NX + x).astype(f32) + x_in[m, t].astype(f32)
+                    z_out[m, t] = total.astype(bf16)
+                    z_copy(m, t).start()
 
     def owned(m):
-        acc[...] = terms[m, 3].astype(f32)
-        for t in range(nz):
-            @pl.when((t == z) & (x == 0))
-            def _(t=t):
-                x_copy(m, t).wait_recv()
-                acc[...] += x_in[m, t].astype(f32)
-
+        acc[...] = terms[m, 3].astype(f32) + x_in[m, z].astype(f32)
         for t in range(1, nz):
             @pl.when(t > z)
             def _(t=t):
@@ -395,11 +370,10 @@
                 remote(block, block, gz_send.at[m, t], gz_recv.at[m, t], t * NX + x, grp).wait_recv()
                 acc[...] += z_in[m, t].astype(f32)
 
-        h = m % HK
-        if m < HK:
-            dv_all[h // 2, grp, :, (h % 2) * DH : (h % 2 + 1) * DH] = acc[...].astype(bf16)
+        if m < 2:
+            dv_all[m, grp] = acc[...].astype(bf16)
         else:
-            dkey[:, h * DH : (h + 1) * DH] = acc[...].astype(bf16)
+            dkey[:, (m - 2) * half : (m - 1) * half] = acc[...].astype(bf16)
 
     def spread(part):
         mine = dv_all.at[part, grp]
@@ -445,37 +419,38 @@
             )
         return copies
 
-    for h in range(HK):
-        softmax(h)
-        forward(h)
-    for h in range(HK):
-        gradients(h)
-        x_stage(h)
-        if h > 0:
-            z_stage(h - 1)
-    z_stage(HK - 1)
-    for h in range(HK):
-        x_stage(HK + h)
+    softmax(0)
+    across_start(values, v_sems, 0)
+    softmax(1)
+    across_start(values, v_sems, 1)
+    softmax(2)
+    softmax(3)
+    gradients(0)
+    gradients(1)
+    x_stage(0)
+    gradients(2)
+    gradients(3)
+    x_stage(1)
+    z_stage(0)
+    x_stage(2)
     owned(0)
-    owned(1)
     to_y, to_c = spread(0)
+    z_stage(1)
+    x_stage(3)
     for copy in hidden:
         copy.wait_recv()
     relayed = relay(0, to_y)
-    z_stage(HK)
     to_c.wait_recv()
     relayed.wait_recv()
     weight_x(0)
-    owned(2)
-    owned(3)
+    owned(1)
     to_y, to_c = spread(1)
-    z_stage(HK + 1)
+    z_stage(2)
     relayed = relay(1, to_y)
-    z_stage(HK + 2)
     to_c.wait_recv()
     relayed.wait_recv()
     weight_x(1)
-    z_stage(HK + 3)
+    z_stage(3)
     copies = weight_z(0)
     width = hidden_ref.shape[1] // 4
     weight = jnp.concatenate([w_all[i].reshape(hidden_ref.shape[1], quarter) for i in range(4)], axis=1)
@@ -483,8 +458,8 @@
     for i in range(4):
         dhidden[:, i * width : (i + 1) * width] = nt(dv_low, weight[i * width : (i + 1) * width, :]).astype(bf16)
     copies += weight_z(1)
-    for h in range(HK):
-        owned(HK + h)
+    owned(2)
+    owned(3)
     for copy in copies:
         copy.wait_recv()
     for part in range(2):
@@ -493,20 +468,16 @@
             total = total + pz_in[part, 1, d - 1].astype(f32)
         dweight[:, part * half : (part + 1) * half] = total
 
-    for h in range(HK):
-        up, across = k_sems(h)
-        sent(keys[h].at[leaf], keys[h], up, across)
-        up, across = v_sems(h)
-        sent(values[h].at[leaf], values[h], up, across)
-    for m in range(2 * HK):
-        for t in range(nz):
-            @pl.when((t < z) | ((t == z) & (x == 1)))
-            def _(t=t, m=m):
-                x_copy(m, t).wait_send()
-        for t in range(nz - 1):
-            @pl.when(t < z)
-            def _(t=t, m=m):
-                z_copy(m, t).wait_send()
+    for part in range(2):
+        sent(keys, k_sems, part)
+        sent(values, v_sems, part)
+    for m in range(4):
+        for k in range(nz):
+            @pl.when(z == k)
+            def _(k=k, m=m):
+                x_copy(m, k).wait_send()
+                for t in range(k):
+                    z_copy(m, t).wait_send()
     for copy in pending:
         copy.wait_send()
     for h in range(HK):
@@ -515,28 +486,18 @@
 
 
 def hand_over_kernel(*refs):
-    sems = refs[10]
-    copies = [pltpu.make_async_copy(refs[i], refs[5 + i], sems.at[i]) for i in range(2, 5)]
-    half = refs[0].shape[0] // 2
-    for i in range(2):
-        for j in range(2):
-            rows = pl.ds(j * half, half)
-            sem = sems.at[i if j == 0 else 5 + i]
-            copies.append(pltpu.make_async_copy(refs[i].at[rows], refs[5 + i].at[rows], sem))
-    for copy in copies:
-        copy.start()
-    for copy in copies:
-        copy.wait()
+    for i in range(5):
+        refs[5 + i][...] = refs[i][...]
 
 
 def hand_over(*arrays):
-    anywhere = pl.BlockSpec(memory_space=pl.ANY)
+    blocks = [pl.BlockSpec((a.shape[0], a.shape[1] // HK), lambda i: (0, i)) for a in arrays]
     return pl.pallas_call(
         hand_over_kernel,
         out_shape=[jax.ShapeDtypeStruct(a.shape, a.dtype) for a in arrays],
-        in_specs=[anywhere] * 5,
-        out_specs=[anywhere] * 5,
-        scratch_shapes=[pltpu.SemaphoreType.DMA((7,))],
+        grid=(HK,),
+        in_specs=blocks,
+        out_specs=blocks,
         compiler_params=pltpu.CompilerParams(vmem_limit_bytes=VMEM_LIMIT),
     )(*arrays)
 
@@ -571,18 +532,18 @@
             held((n_grp, NX, nz, rows, seg), bf16),
             held((4, nz, NX, ny, NC, rows, width // 4), bf16),
         ]
-        + [held((n_leaf, seg, DH), bf16)] * (2 * HK)
+        + [held((n_leaf, seg, half), bf16)] * 4
         + [
             held((n_leaf, 8, 128), jnp.int32),
             held((8, 128), jnp.int32),
             pltpu.SMEM((n_leaf, 128), jnp.int32),
             held((4 * seg, 2 * seg), f32),
             held((HQ // 2, 4 * seg, 2 * seg), f32),
-            held((2 * HK, 4, seg, DH), bf16),
+            held((4, 4, seg, half), bf16),
         ]
-        + [held((2 * HK, nz, seg, DH), bf16)] * 4
+        + [held((4, nz, seg, half), bf16)] * 4
         + [
-            held((seg, DH), f32),
+            held((seg, half), f32),
             held((n_grp, NX, nz, rows, seg), bf16),
             held((2, n_grp, seg, half), bf16),
             held((2, nz, rows, half), bf16),
@@ -596,11 +557,9 @@
         + pairs(2, nz - 1)
         + pairs(2, 4)
         + pairs(2, 5)
-        + pairs(HK, nz - 1)
-        + pairs(HK, nz)
-        + pairs(HK, nz - 1)
-        + pairs(HK, nz)
-        + pairs(2 * HK, nz) * 2
+        + (pairs(2, nz - 1) + pairs(2)) * 2
+        + pairs(4)
+        + pairs(4, nz)
         + pairs(n_grp - 1)
         + pairs(2, 3)
         + pairs(2)

time: 201 us -> 98.5 us (0.49)
  Pallas kernels: 199 us -> 96.8 us
    pallas_call x1, Pallas kernels: 109 us -> 4.33 us  [hand_over(): pl.pallas_call(hand_over_kernel, out_shape=[jax.ShapeDtypeStruct(a.shape,...]
    pallas_call x1, Pallas kernels: 89.8 us -> 92.5 us  [fast_shards(): pl.pallas_call(functools.partial(tree_kernel, n_leaf, n_grp), out_shape=[...]
where the time goes in v5:
time: 98.5 us; the launch traced here: 98.2 us
  Pallas kernels  96.8 us (98%)
  between operations  1.44 us (1%)
    pallas_call x1, Pallas kernels, fast_shards(): pl.pallas_call(functools.partial(tree_kernel, n_leaf, n_grp), out_shape=[...  92.5 us
    pallas_call x1, Pallas kernels, hand_over(): pl.pallas_call(hand_over_kernel, out_shape=[jax.ShapeDtypeStruct(a.shape,...  4.33 us

profile of v5, /device:TPU:0, one launch (start us, length us, event | category | flops | bytes accessed | tf_op | source)
XLA Modules:
  0.0 98.2 jit_solution(14646693958797611171)
XLA Ops:
  1.3 92.5 %shard_map.101 = (bf16[128,5120]{1,0:T(8,128)(2,1)}, bf16[128,5120]{1,0:T(8,128)(2,1)}, bf16[128,512]{1,0:T(8,128)(2,1)}, bf16[128,2560]{1,0:T(8,128)(2,1)}, f32[80,512]{1,0:T(8,128)}) custom-call(s32[1,1]{1,0:T(1,128)S(6)} %copy.11.parent_ref, bf16[80,512]{1,0:T(8,128)(2,1)} %w_ref.1, bf16[128,512]{1,0:T(8,128)(2,1)} %bitcast.14, ...), custom_call_target="tpu_custom_call" | custom-call | flops 5033164800 | bytes 10000000 | tf_op jit(solution)/shard_map/pallas_call | solution.py:516
  93.7 4.3 %shard_map.102 = (bf16[128,5120]{1,0:T(8,128)(2,1)}, bf16[128,5120]{1,0:T(8,128)(2,1)}, bf16[128,512]{1,0:T(8,128)(2,1)}, bf16[128,2560]{1,0:T(8,128)(2,1)}, f32[80,512]{1,0:T(8,128)}) custom-call(bf16[128,5120]{1,0:T(8,128)(2,1)} %get-tuple-element.15.refs_0_, bf16[128,5120]{1,0:T(8,128)(2,1)} %get-tuple-element.16.refs_1_, ...), custom_call_target="tpu_custom_call" | custom-call | tf_op jit(solution)/shard_map/pallas_call | solution.py:495
